TPU v7x, 32 devices: a whole 2x2x4 slice. The times are simulated.
32 devices in a mesh: band: 8 (over z, y), lon: 4 (over x, core).
Axes of the slice: x: 2, y: 2, z: 4, core: 2. Of those that a mesh axis runs over, the one named last changes fastest.
Arguments:
- state: bfloat16 [822, 16, 2048], P(None, 'band', 'lon'), may hold values from -6 to 6
- kernel: float32 [822, 3, 3], replicated, may hold values from -6 to 6
- w_state: bfloat16 [256, 822], replicated, may hold values from -0.21875 to 0.21875
- w_conv: bfloat16 [256, 822], replicated, may hold values from -0.21875 to 0.21875
- w_adj: bfloat16 [256, 822], replicated, may hold values from -0.875 to 0.875
- bias_in: float32 [256], replicated, may hold values from -6 to 6
- w_out: bfloat16 [822, 256], replicated, may hold values from -0.375 to 0.375
- obs_op: bfloat16 [96, 822], replicated, may hold values from -0.078125 to 0.078125
- observations: float32 [96, 8, 512], P(None, 'band', 'lon'), may hold values from -12 to 12
- obs_mask: int32 [96, 8, 512], P(None, 'band', 'lon'), may hold values 0 or 1
- dual_in: bfloat16 [96, 8, 512], P(None, 'band', 'lon'), may hold values from -6 to 6
- dual_res: bfloat16 [256, 96], replicated, may hold values from -0.625 to 0.625
- dual_prev: bfloat16 [256, 96], replicated, may hold values from -0.625 to 0.625
- dual_bias: float32 [256], replicated, may hold values from -6 to 6
- dual_out_w: bfloat16 [96, 256], replicated, may hold values from -0.375 to 0.375
- footprint: int32 [8, 4, 8, 4], P('band', 'lon'), may hold values from 0 to 7, all different within a row; in each aligned block of 8 rows (0 to 7, 8 to 15, ..., all dimensions but the last counted through in order) at most 8 rows name the same one
Outputs:
- state_out: bfloat16 [822, 16, 2048], P(None, 'band', 'lon')
- dual_out: bfloat16 [96, 8, 512], P(None, 'band', 'lon')
Inputs may be any that keep to these rules, and one draw needn't show every extreme that they name: `footprint`: within the 8 column blocks of one pair (b, l), the 4 entries of a block differ, and no value appears more than 8 times; in some pairs one value appears exactly 8 times.
All inputs are finite; a program needn't handle non-finite values. No bound on the sum of `obs_mask` on one device may be relied on, other than what follows from the above.
Results may differ from a plain program's by a relative error of at most 0.0075.
Values may be sent and summed in bfloat16 or wider, within the bound.
A program may use at most 64 MiB of HBM per device.

v0:
```python
import jax
import jax.numpy as jnp
from jax import lax
from jax.sharding import PartitionSpec as P

PIX = 128
TOP = 4


def extended(value, sides, width, wrap):
    for axis, dim in sides:
        count, length = (lax.axis_size(axis), value.shape[dim])
        up = [(i, (i + 1) % count) for i in range(count if wrap else count - 1)]
        down = [(j, i) for i, j in up]
        last = lax.slice_in_dim(value, length - width, length, axis=dim)
        initial = lax.slice_in_dim(value, 0, width, axis=dim)
        before = lax.ppermute(last, axis, up)
        after = lax.ppermute(initial, axis, down)
        value = jnp.concatenate([before, value, after], axis=dim)
    return value


def on_device(
    state,
    kernel,
    w_state,
    w_conv,
    w_adj,
    bias_in,
    w_out,
    obs_op,
    observations,
    obs_mask,
    dual_in,
    dual_res,
    dual_prev,
    dual_bias,
    dual_out_w,
    footprint,
):
    channels, lat_rows, lon_cols = state.shape
    radiance = obs_op.shape[0]
    owners = lax.axis_size("band")
    nblocks = lat_rows * lon_cols // PIX
    routes = footprint.reshape(nblocks, TOP)
    targets = jnp.arange(owners, dtype=jnp.int32)
    member = (routes[:, :, None] == targets[None, None, :]).astype(jnp.int32)
    cover = jnp.sum(member, axis=1).astype(jnp.bfloat16)
    columns = state.reshape(channels, nblocks, PIX)
    projected = jnp.einsum(
        "rc,ckp->krp", obs_op, columns, preferred_element_type=jnp.float32
    ).astype(jnp.bfloat16)
    partial_sums = jnp.einsum(
        "kd,krp->drp", cover, projected, preferred_element_type=jnp.float32
    ).astype(jnp.bfloat16)
    arrived = lax.all_to_all(partial_sums, "band", split_axis=0, concat_axis=0, tiled=True)
    evolved = jnp.sum(arrived, axis=0, dtype=jnp.float32)
    observed = observations.reshape(radiance, PIX)
    valid = obs_mask.reshape(radiance, PIX)
    dual_now = dual_in.reshape(radiance, PIX)
    departure = jnp.where(valid == 1, evolved - observed, 0.0).astype(jnp.bfloat16)
    pre_dual = jnp.dot(dual_res, departure, preferred_element_type=jnp.float32)
    pre_dual = pre_dual + jnp.dot(dual_prev, dual_now, preferred_element_type=jnp.float32)
    dual_hidden = jax.nn.gelu(pre_dual + dual_bias[:, None]).astype(jnp.bfloat16)
    dual_new = (
        dual_now.astype(jnp.float32)
        + jnp.dot(dual_out_w, dual_hidden, preferred_element_type=jnp.float32)
    ).astype(jnp.bfloat16)
    everyone = lax.all_gather(dual_new[:, None, :], "band", axis=1, tiled=True)
    back_sum = jnp.einsum("kd,rdp->krp", cover, everyone, preferred_element_type=jnp.float32)
    back = back_sum.astype(jnp.bfloat16)
    adjoint = jnp.einsum("rc,krp->ckp", obs_op, back, preferred_element_type=jnp.float32).astype(
        jnp.bfloat16
    )
    adjoint = adjoint.reshape(channels, lat_rows * lon_cols)
    widened = extended(state, (("lon", 2),), 1, True)
    padded = extended(widened, (("band", 1),), 1, False)
    filtered = jnp.zeros((channels, lat_rows, lon_cols), jnp.float32)
    for a in range(3):
        for e in range(3):
            filtered = filtered + kernel[:, a, e][:, None, None] * padded[
                :, a : a + lat_rows, e : e + lon_cols
            ].astype(jnp.float32)
    filtered = filtered.astype(jnp.bfloat16).reshape(channels, lat_rows * lon_cols)
    flat_state = state.reshape(channels, lat_rows * lon_cols)
    pre_state = jnp.dot(w_state, flat_state, preferred_element_type=jnp.float32)
    pre_state = pre_state + jnp.dot(w_conv, filtered, preferred_element_type=jnp.float32)
    pre_state = pre_state + jnp.dot(w_adj, adjoint, preferred_element_type=jnp.float32)
    hidden = jax.nn.gelu(pre_state + bias_in[:, None]).astype(jnp.bfloat16)
    updated = flat_state.astype(jnp.float32) + jnp.dot(
        w_out, hidden, preferred_element_type=jnp.float32
    )
    state_out = updated.astype(jnp.bfloat16).reshape(channels, lat_rows, lon_cols)
    return (state_out, dual_new.reshape(radiance, 1, PIX))


def solution(mesh):
    in_specs = (
        P(None, "band", "lon"),
        P(),
        P(),
        P(),
        P(),
        P(),
        P(),
        P(),
        P(None, "band", "lon"),
        P(None, "band", "lon"),
        P(None, "band", "lon"),
        P(),
        P(),
        P(),
        P(),
        P("band", "lon", None, None),
    )
    out_specs = (P(None, "band", "lon"), P(None, "band", "lon"))
    return jax.shard_map(
        on_device, mesh=mesh, in_specs=in_specs, out_specs=out_specs, check_vma=False
    )
```

profile of v0, /device:TPU:0, one launch (start us, length us, event | category | flops | bytes accessed | tf_op | source)
XLA Modules:
  0.0 123.8 jit_solution(10194226473613889047)
XLA Ops:
  0.7 4.7 %copy.58 = bf16[822,2,512]{0,2,1:T(8,128)(2,1)S(1)} copy(bf16[822,2,512]{2,1,0:T(2,128)(2,1)} %param.16) | data formatting | bytes 3366912 | tf_op args[0]
  6.4 1.9 %collective-permute-start.1 = (bf16[822,2,1]{0,2,1:T(2,128)(2,1)}, bf16[822,2,1]{0,2,1:T(2,128)(2,1)S(1)}, u32[]{:S(2)}, u32[]{:S(2)}) collective-permute-start(bf16[822,2,1]{0,2,1:T(2,128)(2,1)} %get-tuple-element.16), channel_id=1, source_target_pairs={{1,0},{2,1},{3,2},{0,3},{5,4},{6,5},{7,6},{4,7},{9,8},{10,9},{11,1... | collective-permute-start | bytes 9872 | tf_op jit(solution)/shard_map/ppermute | solution.py:18
  8.3 5.0 %reshape.35 = bf16[822,8,128]{2,1,0:T(8,128)(2,1)} reshape(bf16[822,2,512]{2,1,0:T(2,128)(2,1)} %param.16) | data formatting | bytes 3366912 | tf_op jit(solution)/shard_map/reshape | solution.py:49
  13.4 1.9 %fusion.10 = bf16[8,96,128]{2,1,0:T(8,128)(2,1)S(1)} fusion(bf16[822,8,128]{2,1,0:T(8,128)(2,1)} %reshape.35, bf16[96,822]{1,0:T(8,128)(2,1)S(1)} %copy-done.5), kind=kOutput, calls=%fused_computation.21 | convolution fusion | flops 161710080 | bytes 2037888 | tf_op jit(solution)/shard_map/rc,ckp->krp/dot_general | solution.py:50
  15.5 0.7 copy.68
  16.3 6.6 %all-to-all-start = ((bf16[8,96,128]{2,1,0:T(8,128)(2,1)}), bf16[8,96,128]{2,1,0:T(8,128)(2,1)S(1)}, u32[]{:S(2)}, u32[]{:S(2)}) async-start(bf16[8,96,128]{2,1,0:T(8,128)(2,1)} %copy.68), calls=%async_computation | async-start | bytes 393216 | tf_op jit(solution)/shard_map/all_to_all | solution.py:56
  22.9 2.8 %pad.19 = bf16[824,2,512]{2,1,0:T(2,128)(2,1)S(1)} pad(bf16[822,2,512]{2,1,0:T(2,128)(2,1)} %param.16, bf16[]{:T(256)} %constant.37), padding=0_2x0_0x0_0 | pad | bytes 3371010
  26.2 0.7 broadcast_compare_fusion
  27.0 0.8 fusion.67
  27.8 0.9 fusion.47
  28.6 0.7 slice_reduce_fusion.8
  29.8 1.4 %fusion.65 = (bf16[822,1,514]{0,2,1:T(8,128)(2,1)}, bf16[822,1,514]{0,2,1:T(8,128)(2,1)}) fusion(bf16[822,2,514]{0,2,1:T(8,128)(2,1)S(1)} %pad_maximum_fusion.1), kind=kLoop, calls=%fused_computation.89 | loop fusion | bytes 3380064 | tf_op jit(solution)/shard_map/slice | solution.py:15
  31.2 4.8 %collective-permute-start.2 = (bf16[822,1,514]{0,2,1:T(8,128)(2,1)}, bf16[822,1,514]{0,2,1:T(8,128)(2,1)}, u32[]{:S(2)}, u32[]{:S(2)}) collective-permute-start(bf16[822,1,514]{0,2,1:T(8,128)(2,1)} %get-tuple-element.11), channel_id=1, source_target_pairs={{0,4},{4,8},{8,12},{12,16},{16,20},{20,24},{24,28},{1,5},{5,9},{9,... | collective-permute-start | bytes 2535056 | tf_op jit(solution)/shard_map/ppermute | solution.py:17
  36.1 1.3 %collective-permute-start.3 = (bf16[822,1,514]{0,2,1:T(8,128)(2,1)}, bf16[822,1,514]{0,2,1:T(8,128)(2,1)}, u32[]{:S(2)}, u32[]{:S(2)}) collective-permute-start(bf16[822,1,514]{0,2,1:T(8,128)(2,1)} %get-tuple-element.12), channel_id=1, source_target_pairs={{4,0},{8,4},{12,8},{16,12},{20,16},{24,20},{28,24},{5,1},{9,5},{13... | collective-permute-start | bytes 2535056 | tf_op jit(solution)/shard_map/ppermute | solution.py:18
  37.4 0.6 convert_reduce_fusion
  38.0 1.4 %fusion.16 = bf16[96,128]{1,0:T(8,128)(2,1)S(1)} fusion(bf16[96,256]{1,0:T(8,128)(2,1)} %param.30, f32[256,128]{0,1:T(8,128)} %fusion.47, bf16[256,96]{0,1:T(8,128)(2,1)} %param.27, f32[256]{0:T(256)} %param.29, f32[96,128]{1,0:T(8,128)} %convert_reduce_fusion, f32[96,128]{1,0:T(8,128)} %bitcast.94, pred[96,1,128]{2,1,0:T(4,128)(4,1)} %broadcast_compare_fusion, ...), kind=kOutput, calls=%fused_computation.27 | convolution fusion | flops 13017088 | bytes 390144 | tf_op jit(solution)/shard_map/dot_general | solution.py:67
  39.4 58.9 %all-gather = bf16[96,1024]{1,0:T(8,128)(2,1)S(1)} all-gather(bf16[96,128]{1,0:T(8,128)(2,1)S(1)} %fusion.16), channel_id=2, replica_groups=mesh['band'=8,'lon'=4] {'band'}, dimensions={1}, use_global_device_ids=true | all-gather | bytes 221184 | tf_op jit(solution)/shard_map/all_gather | solution.py:69
  98.6 1.6 %fusion.3 = bf16[822,8,128]{2,0,1:T(8,128)(2,1)S(1)} fusion(bf16[8,96,128]{2,0,1:T(8,128)(2,1)S(1)} %convolution_convert_fusion.1, bf16[96,822]{1,0:T(8,128)(2,1)} %param.23), kind=kOutput, calls=%fused_computation.12 | convolution fusion | flops 162453504 | bytes 2037888 | tf_op jit(solution)/shard_map/rc,krp->ckp/dot_general | solution.py:72
  100.5 1.7 %copy.81 = bf16[103,8,8,128]{3,1,2,0:T(8,128)(2,1)} copy(bf16[103,8,8,128]{3,2,1,0:T(8,128)(2,1)S(1)} %bitcast.87) | data formatting | bytes 3375104
  102.3 4.8 %maximum_maximum_fusion = (bf16[822,3,514]{0,2,1:T(8,128)(2,1)S(1)}, bf16[822,3,514]{0,2,1:T(8,128)(2,1)S(1)}) fusion(bf16[822,2,1]{0,2,1:T(2,128)(2,1)S(1)} %collective-permute-done.1, bf16[822,2,512]{0,2,1:T(8,128)(2,1)S(1)} %copy.58, bf16[822,2,1]{0,2,1:T(2,128)(2,1)S(1)} %collective-permute-done, bf16[822,1,514]{0,2,1:T(8,128)(2,1)} %collective-permute-done.2, ...), kind=kLoop, calls=%fused_computation.3 | loop fusion | flops 20280384 | bytes 8450160 | tf_op jit(solution)/shard_map/concatenate | solution.py:19
  107.1 5.2 %add_convert_fusion = bf16[822,2,512]{0,2,1:T(8,128)(2,1)S(1)} fusion(bf16[822,2,512]{0,2,1:T(8,128)(2,1)S(1)} %copy.58, bf16[822,3,514]{0,2,1:T(8,128)(2,1)S(1)} %get-tuple-element.14, bf16[822,2,1]{0,2,1:T(2,128)(2,1)S(1)} %collective-permute-done.1, bf16[822,2,1]{0,2,1:T(2,128)(2,1)S(1)} %collective-permute-done, ...), kind=kLoop, calls=%fused_computation | loop fusion | flops 27777024 | bytes 13503816 | tf_op jit(solution)/shard_map/convert_element_type | solution.py:84
  112.3 1.7 %fusion.6 = f32[256,1024]{1,0:T(8,128)} fusion(f32[256,1024]{1,0:T(8,128)S(1)} %fusion.67, bf16[822,1024]{0,1:T(8,128)(2,1)S(1)} %bitcast.84, bf16[256,822]{0,1:T(8,128)(2,1)S(1)} %copy-done.4), kind=kOutput, calls=%fused_computation.17 | convolution fusion | flops 431226880 | bytes 4201472 | tf_op jit(solution)/shard_map/dot_general | solution.py:87
  114.1 4.6 %fusion = bf16[822,1024]{1,0:T(8,128)(2,1)} fusion(bf16[822,1024]{1,0:T(8,128)(2,1)S(1)} %bitcast.86, bf16[822,256]{1,0:T(8,128)(2,1)S(1)} %copy-done, f32[256,1024]{1,0:T(8,128)} %fusion.6, bf16[822,1024]{1,0:T(8,128)(2,1)} %bitcast.89, bf16[256,822]{0,1:T(8,128)(2,1)} %param.20, f32[256]{0:T(256)S(1)} %copy-done.19), kind=kOutput, calls=%fused_computation.2 | convolution fusion | flops 867338240 | bytes 6941696 | tf_op jit(solution)/shard_map/dot_general | solution.py:90
  118.6 5.1 %reshape.38 = bf16[822,2,512]{2,1,0:T(2,128)(2,1)} reshape(bf16[822,1024]{1,0:T(8,128)(2,1)} %fusion) | data formatting | bytes 3366912 | tf_op jit(solution)/shard_map/reshape | solution.py:93
  (55 shorter events, 3.0 us)
Async XLA Ops:
  0.6 113.4 %copy-start = (bf16[822,256]{1,0:T(8,128)(2,1)S(1)}, bf16[822,256]{1,0:T(8,128)(2,1)}, u32[]{:S(2)}) copy-start(bf16[822,256]{1,0:T(8,128)(2,1)} %param.22) | copy-start | bytes 1262596
  0.6 12.7 %copy-start.18 = (s32[1,1,8,4]{2,3,1,0:T(4,128)S(1)}, s32[1,1,8,4]{2,3,1,0:T(4,128)}, u32[]{:S(2)}) copy-start(s32[1,1,8,4]{2,3,1,0:T(4,128)} %param.31) | copy-start | bytes 388
  0.7 12.7 %copy-start.5 = (bf16[96,822]{1,0:T(8,128)(2,1)S(1)}, bf16[96,822]{1,0:T(8,128)(2,1)}, u32[]{:S(2)}) copy-start(bf16[96,822]{1,0:T(8,128)(2,1)} %param.23) | copy-start | bytes 473476
  6.0 23.3 %collective-permute-start = (bf16[822,2,1]{0,2,1:T(2,128)(2,1)}, bf16[822,2,1]{0,2,1:T(2,128)(2,1)S(1)}, u32[]{:S(2)}, u32[]{:S(2)}) collective-permute-start(bf16[822,2,1]{0,2,1:T(2,128)(2,1)} %get-tuple-element.15), channel_id=1, source_target_pairs={{0,1},{1,2},{2,3},{3,0},{4,5},{5,6},{6,7},{7,4},{8,9},{9,10},{10,1... | collective-permute-start | bytes 9872 | tf_op jit(solution)/shard_map/ppermute | solution.py:17
  6.4 22.9 %collective-permute-start.1 = (bf16[822,2,1]{0,2,1:T(2,128)(2,1)}, bf16[822,2,1]{0,2,1:T(2,128)(2,1)S(1)}, u32[]{:S(2)}, u32[]{:S(2)}) collective-permute-start(bf16[822,2,1]{0,2,1:T(2,128)(2,1)} %get-tuple-element.16), channel_id=1, source_target_pairs={{1,0},{2,1},{3,2},{0,3},{5,4},{6,5},{7,6},{4,7},{9,8},{10,9},{11,1... | collective-permute-start | bytes 9872 | tf_op jit(solution)/shard_map/ppermute | solution.py:18
  16.3 21.1 %all-to-all-start = ((bf16[8,96,128]{2,1,0:T(8,128)(2,1)}), bf16[8,96,128]{2,1,0:T(8,128)(2,1)S(1)}, u32[]{:S(2)}, u32[]{:S(2)}) async-start(bf16[8,96,128]{2,1,0:T(8,128)(2,1)} %copy.68), calls=%async_computation | async-start | bytes 393216 | tf_op jit(solution)/shard_map/all_to_all | solution.py:56
  22.9 3.3 %copy-start.6 = (s32[96,1,128]{2,1,0:T(1,128)S(1)}, s32[96,1,128]{2,1,0:T(1,128)}, u32[]{:S(2)}) copy-start(s32[96,1,128]{2,1,0:T(1,128)} %param.25) | copy-start | bytes 147460
  22.9 4.1 %copy-start.3 = (bf16[256,822]{0,1:T(8,128)(2,1)S(1)}, bf16[256,822]{0,1:T(8,128)(2,1)}, u32[]{:S(2)}) copy-start(bf16[256,822]{0,1:T(8,128)(2,1)} %param.18) | copy-start | bytes 1262596
  25.7 2.0 %copy-start.7 = (bf16[256,96]{0,1:T(8,128)(2,1)S(1)}, bf16[256,96]{0,1:T(8,128)(2,1)}, u32[]{:S(2)}) copy-start(bf16[256,96]{0,1:T(8,128)(2,1)} %param.28) | copy-start | bytes 147460
  25.7 2.0 %copy-start.8 = (bf16[96,1,128]{2,0,1:T(8,128)(2,1)S(1)}, bf16[96,1,128]{2,0,1:T(8,128)(2,1)}, u32[]{:S(2)}) copy-start(bf16[96,1,128]{2,0,1:T(8,128)(2,1)} %param.26) | copy-start | bytes 73732
  25.7 2.9 %copy-start.10 = (f32[822,3,3]{0,2,1:T(4,128)S(1)}, f32[822,3,3]{0,2,1:T(4,128)}, u32[]{:S(2)}) copy-start(f32[822,3,3]{0,2,1:T(4,128)} %param.17) | copy-start | bytes 88780
  26.2 3.1 %copy-start.1 = (bf16[103,8,2,512]{3,1,2,0:T(8,128)(2,1)}, bf16[103,8,2,512]{3,1,2,0:T(8,128)(2,1)S(1)}, u32[]{:S(2)}) copy-start(bf16[103,8,2,512]{3,1,2,0:T(8,128)(2,1)S(1)} %copy.79) | copy-start | bytes 5062660
  31.2 71.0 %collective-permute-start.2 = (bf16[822,1,514]{0,2,1:T(8,128)(2,1)}, bf16[822,1,514]{0,2,1:T(8,128)(2,1)}, u32[]{:S(2)}, u32[]{:S(2)}) collective-permute-start(bf16[822,1,514]{0,2,1:T(8,128)(2,1)} %get-tuple-element.11), channel_id=1, source_target_pairs={{0,4},{4,8},{8,12},{12,16},{16,20},{20,24},{24,28},{1,5},{5,9},{9,... | collective-permute-start | bytes 2535056 | tf_op jit(solution)/shard_map/ppermute | solution.py:17
  36.1 66.2 %collective-permute-start.3 = (bf16[822,1,514]{0,2,1:T(8,128)(2,1)}, bf16[822,1,514]{0,2,1:T(8,128)(2,1)}, u32[]{:S(2)}, u32[]{:S(2)}) collective-permute-start(bf16[822,1,514]{0,2,1:T(8,128)(2,1)} %get-tuple-element.12), channel_id=1, source_target_pairs={{4,0},{8,4},{12,8},{16,12},{20,16},{24,20},{28,24},{5,1},{9,5},{13... | collective-permute-start | bytes 2535056 | tf_op jit(solution)/shard_map/ppermute | solution.py:18
  39.4 61.0 %copy-start.9 = (bf16[96,128]{1,0:T(8,128)(2,1)}, bf16[96,128]{1,0:T(8,128)(2,1)S(1)}, u32[]{:S(2)}) copy-start(bf16[96,128]{1,0:T(8,128)(2,1)S(1)} %fusion.16) | copy-start | bytes 73732
  102.2 4.8 %copy-start.11 = (f32[822]{0:T(1024)S(1)}, f32[822]{0:T(1024)}, u32[]{:S(2)}) copy-start(f32[822]{0:T(1024)} %get-tuple-element.4) | copy-start | bytes 9868
  102.2 4.8 %copy-start.12 = (f32[822]{0:T(1024)S(1)}, f32[822]{0:T(1024)}, u32[]{:S(2)}) copy-start(f32[822]{0:T(1024)} %get-tuple-element.5) | copy-start | bytes 9868
  102.2 4.9 %copy-start.13 = (f32[822]{0:T(1024)S(1)}, f32[822]{0:T(1024)}, u32[]{:S(2)}) copy-start(f32[822]{0:T(1024)} %get-tuple-element.6) | copy-start | bytes 9868
  102.2 4.9 %copy-start.14 = (f32[822]{0:T(1024)S(1)}, f32[822]{0:T(1024)}, u32[]{:S(2)}) copy-start(f32[822]{0:T(1024)} %get-tuple-element.7) | copy-start | bytes 9868
  102.2 4.9 %copy-start.15 = (f32[822]{0:T(1024)S(1)}, f32[822]{0:T(1024)}, u32[]{:S(2)}) copy-start(f32[822]{0:T(1024)} %get-tuple-element.8) | copy-start | bytes 9868
  102.2 4.9 %copy-start.16 = (f32[822]{0:T(1024)S(1)}, f32[822]{0:T(1024)}, u32[]{:S(2)}) copy-start(f32[822]{0:T(1024)} %get-tuple-element.9) | copy-start | bytes 9868
  102.2 4.9 %copy-start.17 = (f32[822]{0:T(1024)S(1)}, f32[822]{0:T(1024)}, u32[]{:S(2)}) copy-start(f32[822]{0:T(1024)} %get-tuple-element.10) | copy-start | bytes 9868
  107.1 5.2 %copy-start.4 = (bf16[256,822]{0,1:T(8,128)(2,1)S(1)}, bf16[256,822]{0,1:T(8,128)(2,1)}, u32[]{:S(2)}) copy-start(bf16[256,822]{0,1:T(8,128)(2,1)} %param.19) | copy-start | bytes 1262596
  112.3 1.8 %copy-start.2 = (bf16[103,8,2,512]{3,1,2,0:T(8,128)(2,1)S(1)}, bf16[103,8,2,512]{3,1,2,0:T(8,128)(2,1)}, u32[]{:S(2)}) copy-start(bf16[103,8,2,512]{3,1,2,0:T(8,128)(2,1)} %copy-done.1) | copy-start | bytes 5062660
  (1 other events, 1.8 us)
where the time goes:
time: 124 us
  blocking collectives  58.9 us (48%)
  local copies, waits for them, and re-layouts  23.6 us (19%)
  starting transfers between devices  15.2 us (12%)
  matrix products  13.2 us (11%)
  other arithmetic  11.9 us (10%)
    all_gather x1, blocking collectives, on_device(): everyone = lax.all_gather(dual_new[:, None, :], 'band', axis=1, tiled=True)  58.9 us
    unnamed x46, local copies, waits for them, and re-layouts  9.83 us
    all_to_all x1, starting transfers between devices, on_device(): lax.all_to_all(partial_sums, 'band', split_axis=0, concat_axis=0, tiled=T...  6.65 us
    ppermute x2, starting transfers between devices, extended(): before = lax.ppermute(last, axis, up)  5.3 us
    concatenate x2, other arithmetic, extended(): value = jnp.concatenate([before, value, after], axis=dim)  5.24 us
    convert_element_type x1, other arithmetic, on_device(): filtered.astype(jnp.bfloat16).reshape(channels, lat_rows * lon_cols)  5.16 us
    reshape x1, local copies, waits for them, and re-layouts, on_device(): updated.astype(jnp.bfloat16).reshape(channels, lat_rows, lon_cols)  5.14 us
    reshape x1, local copies, waits for them, and re-layouts, on_device(): columns = state.reshape(channels, nblocks, PIX)  4.96 us
  transfers between devices with their start and end apart: 5, of which 0 were waited for; matrix products, arithmetic and copies ran while one was open for 18% of the time, Pallas kernels for 0%

commit v1 on v0

--- a/solution.py
+++ b/solution.py
@@ -53,6 +53,37 @@
     partial_sums = jnp.einsum(
         "kd,krp->drp", cover, projected, preferred_element_type=jnp.float32
     ).astype(jnp.bfloat16)
+    widened = extended(state, (("lon", 2),), 1, True).astype(jnp.float32)
+
+    def taps(a, row):
+        total = jnp.zeros((channels, lon_cols), jnp.float32)
+        for e in range(3):
+            total = total + kernel[:, a, e][:, None] * widened[:, row, e : e + lon_cols]
+        return total
+
+    def mixed(value):
+        return jnp.dot(w_conv, value.astype(jnp.bfloat16), preferred_element_type=jnp.float32)
+
+    bands = lax.axis_size("band")
+    to_next = [(i, i + 1) for i in range(bands - 1)]
+    to_previous = [(i + 1, i) for i in range(bands - 1)]
+    from_above = lax.ppermute(mixed(taps(0, lat_rows - 1)).astype(jnp.bfloat16), "band", to_next)
+    from_below = lax.ppermute(mixed(taps(2, 0)).astype(jnp.bfloat16), "band", to_previous)
+    rows = []
+    for i in range(lat_rows):
+        own = sum(taps(a, i + a - 1) for a in range(3) if 0 <= i + a - 1 < lat_rows)
+        part = mixed(own)
+        part = part + jnp.dot(w_state, state[:, i], preferred_element_type=jnp.float32)
+        if i == 0:
+            part = part + from_above.astype(jnp.float32)
+        if i == lat_rows - 1:
+            part = part + from_below.astype(jnp.float32)
+        rows.append(part)
+    pre_state = jnp.concatenate(rows, axis=1)
+    flat_state = state.reshape(channels, lat_rows * lon_cols)
+    through = lax.dot_general(
+        w_adj, obs_op, (((1,), (1,)), ((), ())), preferred_element_type=jnp.float32
+    ).astype(jnp.bfloat16)
     arrived = lax.all_to_all(partial_sums, "band", split_axis=0, concat_axis=0, tiled=True)
     evolved = jnp.sum(arrived, axis=0, dtype=jnp.float32)
     observed = observations.reshape(radiance, PIX)
@@ -66,26 +97,11 @@
         dual_now.astype(jnp.float32)
         + jnp.dot(dual_out_w, dual_hidden, preferred_element_type=jnp.float32)
     ).astype(jnp.bfloat16)
-    everyone = lax.all_gather(dual_new[:, None, :], "band", axis=1, tiled=True)
-    back_sum = jnp.einsum("kd,rdp->krp", cover, everyone, preferred_element_type=jnp.float32)
-    back = back_sum.astype(jnp.bfloat16)
-    adjoint = jnp.einsum("rc,krp->ckp", obs_op, back, preferred_element_type=jnp.float32).astype(
-        jnp.bfloat16
-    )
-    adjoint = adjoint.reshape(channels, lat_rows * lon_cols)
-    widened = extended(state, (("lon", 2),), 1, True)
-    padded = extended(widened, (("band", 1),), 1, False)
-    filtered = jnp.zeros((channels, lat_rows, lon_cols), jnp.float32)
-    for a in range(3):
-        for e in range(3):
-            filtered = filtered + kernel[:, a, e][:, None, None] * padded[
-                :, a : a + lat_rows, e : e + lon_cols
-            ].astype(jnp.float32)
-    filtered = filtered.astype(jnp.bfloat16).reshape(channels, lat_rows * lon_cols)
-    flat_state = state.reshape(channels, lat_rows * lon_cols)
-    pre_state = jnp.dot(w_state, flat_state, preferred_element_type=jnp.float32)
-    pre_state = pre_state + jnp.dot(w_conv, filtered, preferred_element_type=jnp.float32)
-    pre_state = pre_state + jnp.dot(w_adj, adjoint, preferred_element_type=jnp.float32)
+    spread = jnp.broadcast_to(dual_new[None], (owners,) + dual_new.shape)
+    everyone = lax.all_to_all(spread, "band", split_axis=0, concat_axis=0, tiled=True)
+    back_sum = jnp.einsum("kd,drp->rkp", cover, everyone, preferred_element_type=jnp.float32)
+    back = back_sum.astype(jnp.bfloat16).reshape(radiance, nblocks * PIX)
+    pre_state = pre_state + jnp.dot(through, back, preferred_element_type=jnp.float32)
     hidden = jax.nn.gelu(pre_state + bias_in[:, None]).astype(jnp.bfloat16)
     updated = flat_state.astype(jnp.float32) + jnp.dot(
         w_out, hidden, preferred_element_type=jnp.float32

time: 124 us -> 70.6 us (0.57)
  blocking collectives: 58.9 us -> 0 us
  matrix products: 13.2 us -> 28.4 us
  other arithmetic: 11.9 us -> 1.16 us
  local copies, waits for them, and re-layouts: 23.6 us -> 16.7 us
  starting transfers between devices: 15.2 us -> 21 us
  waiting for transfers between devices: 0.01 us -> 1.68 us
    all_gather x1 -> x0, blocking collectives: 58.9 us -> none  [on_device(): everyone = lax.all_gather(dual_new[:, None, :], 'band', axis=1, tiled=True)]
    dot_general x4 -> x8, matrix products: 4.25 us -> 21.7 us  [the longest x4 15.6 us: mixed(): jnp.dot(w_conv, value.astype(jnp.bfloat16), preferred_element_type=jnp.fl...]
    all_to_all x0 -> x1, starting transfers between devices: none -> 6.57 us  [on_device(): lax.all_to_all(spread, 'band', split_axis=0, concat_axis=0, tiled=True)]
    ppermute x0 -> x2, starting transfers between devices: none -> 5.4 us  [the longest x1 3.93 us: on_device(): lax.ppermute(mixed(taps(0, lat_rows - 1)).astype(jnp.bfloat16), 'band', t...]
    concatenate x2 -> x0, other arithmetic: 5.24 us -> none  [extended(): value = jnp.concatenate([before, value, after], axis=dim)]
    ppermute x2 -> x1, starting transfers between devices: 5.3 us -> 0.45 us  [extended(): before = lax.ppermute(last, axis, up)]
    convert_element_type x1, other arithmetic: 5.16 us -> 0.99 us  [on_device(): widened = extended(state, (('lon', 2),), 1, True).astype(jnp.float32)]
    unnamed x46 -> x39, local copies, waits for them, and re-layouts: 9.83 us -> 6.69 us
  transfers between devices with their start and end apart: 5 -> 6, of which waited for: 0 -> 1; matrix products, arithmetic and copies ran while one was open for 18% -> 45% of each run, Pallas kernels for 0% -> 0%
where the time goes in v1:
time: 70.6 us; the launch traced here: 70 us
  matrix products  28.4 us (40%)
  starting transfers between devices  21 us (30%)
  local copies, waits for them, and re-layouts  16.7 us (24%)
  waiting for transfers between devices  1.68 us (2%)
  other arithmetic  1.16 us (2%)
  between operations  0.97 us (1%)
    dot_general x4, matrix products, mixed(): jnp.dot(w_conv, value.astype(jnp.bfloat16), preferred_element_type=jnp.fl...  15.6 us
    unnamed x39, local copies, waits for them, and re-layouts  6.69 us
    all_to_all x1, starting transfers between devices, on_device(): lax.all_to_all(partial_sums, 'band', split_axis=0, concat_axis=0, tiled=T...  6.59 us
    all_to_all x1, starting transfers between devices, on_device(): lax.all_to_all(spread, 'band', split_axis=0, concat_axis=0, tiled=True)  6.57 us
    reshape x1, local copies, waits for them, and re-layouts, on_device(): updated.astype(jnp.bfloat16).reshape(channels, lat_rows, lon_cols)  5.14 us
    dot_general x2, matrix products, on_device(): jnp.dot(w_state, state[:, i], preferred_element_type=jnp.float32)  4.24 us
    dot_general x1, matrix products, on_device(): jnp.dot(w_out, hidden, preferred_element_type=jnp.float32)  4 us
    ppermute x1, starting transfers between devices, on_device(): lax.ppermute(mixed(taps(0, lat_rows - 1)).astype(jnp.bfloat16), 'band', t...  3.93 us
  transfers between devices with their start and end apart: 6, of which 1 were waited for; matrix products, arithmetic and copies ran while one was open for 45% of the time, Pallas kernels for 0%

profile of v1, /device:TPU:0, one launch (start us, length us, event | category | flops | bytes accessed | tf_op | source)
XLA Modules:
  0.0 70.0 jit_solution(11011378661050902727)
XLA Ops:
  0.6 1.8 %copy.67 = bf16[822,2,512]{2,0,1:T(8,128)(2,1)S(1)} copy(bf16[822,2,512]{2,1,0:T(2,128)(2,1)} %param.16) | data formatting | bytes 3366912 | tf_op args[0]
  2.4 1.2 %copy-done.2 = bf16[822,2,512]{2,0,1:T(8,128)(2,1)} copy-done((bf16[822,2,512]{2,0,1:T(8,128)(2,1)}, bf16[822,2,512]{2,0,1:T(8,128)(2,1)S(1)}, u32[]{:S(2)}) %copy-start.2) | copy-done | bytes 1683480
  3.6 1.1 %fusion.74 = (bf16[822,2,1]{2,0,1:T(8,128)(2,1)}, bf16[822,2,1]{2,0,1:T(8,128)(2,1)}) fusion(bf16[822,2,512]{2,0,1:T(8,128)(2,1)S(1)} %copy.67), kind=kLoop, calls=%fused_computation.107 | loop fusion | bytes 13152 | tf_op jit(solution)/shard_map/slice | solution.py:15
  5.2 2.0 %collective-permute-start.1 = (bf16[822,2,1]{2,0,1:T(8,128)(2,1)}, bf16[822,2,1]{2,0,1:T(8,128)(2,1)S(1)}, u32[]{:S(2)}, u32[]{:S(2)}) collective-permute-start(bf16[822,2,1]{2,0,1:T(8,128)(2,1)} %get-tuple-element.12), channel_id=1, source_target_pairs={{1,0},{2,1},{3,2},{0,3},{5,4},{6,5},{7,6},{4,7},{9,8},{10,9},{11,1... | collective-permute-start | bytes 9872 | tf_op jit(solution)/shard_map/ppermute | solution.py:18
  7.1 2.3 %reshape.42 = bf16[822,8,128]{2,1,0:T(8,128)(2,1)} reshape(bf16[822,2,512]{2,1,0:T(2,128)(2,1)S(1)} %copy-done.1) | data formatting | bytes 3366912 | tf_op jit(solution)/shard_map/reshape | solution.py:49
  9.5 1.9 %fusion.12 = bf16[8,96,128]{2,1,0:T(8,128)(2,1)S(1)} fusion(bf16[822,8,128]{2,1,0:T(8,128)(2,1)} %reshape.42, bf16[96,822]{1,0:T(8,128)(2,1)S(1)} %copy-done.5), kind=kOutput, calls=%fused_computation.29 | convolution fusion | flops 161710080 | bytes 2037888 | tf_op jit(solution)/shard_map/rc,ckp->krp/dot_general | solution.py:50
  11.7 0.7 %copy.77 = bf16[8,96,128]{2,1,0:T(8,128)(2,1)} copy(bf16[8,96,128]{2,0,1:T(8,128)(2,1)S(1)} %convolution_convert_fusion.3) | data formatting | bytes 393216 | tf_op jit(solution)/shard_map/convert_element_type | solution.py:55
  12.4 6.6 %all-to-all-start = ((bf16[8,96,128]{2,1,0:T(8,128)(2,1)}), bf16[8,96,128]{2,1,0:T(8,128)(2,1)S(1)}, u32[]{:S(2)}, u32[]{:S(2)}) async-start(bf16[8,96,128]{2,1,0:T(8,128)(2,1)} %copy.77), calls=%async_computation | async-start | bytes 393216 | tf_op jit(solution)/shard_map/all_to_all | solution.py:87
  19.1 1.9 %fusion.30 = f32[256,512]{0,1:T(8,128)S(1)} fusion(bf16[256,822]{0,1:T(8,128)(2,1)} %param.18, bf16[822,2,512]{2,0,1:T(8,128)(2,1)} %copy-done.2), kind=kOutput, calls=%fused_computation.51 | convolution fusion | flops 215482368 | bytes 1789952 | tf_op jit(solution)/shard_map/dot_general | solution.py:76
  21.0 2.3 %fusion.29 = f32[256,512]{0,1:T(8,128)} fusion(bf16[256,822]{0,1:T(8,128)(2,1)} %param.18, bf16[822,2,512]{2,0,1:T(8,128)(2,1)S(1)} %copy-done.3), kind=kOutput, calls=%fused_computation.49 | convolution fusion | flops 215482368 | bytes 1788928 | tf_op jit(solution)/shard_map/dot_general | solution.py:76
  23.7 1.2 %pad.5 = f32[824,2,512]{2,1,0:T(2,128)S(1)} pad(bf16[822,2,512]{2,1,0:T(2,128)(2,1)S(1)} %copy-done.1, f32[]{:T(128)} %constant.9.clone.1), padding=0_2x0_0x0_0 | pad | bytes 5058564
  24.9 2.5 %copy.88 = f32[103,8,2,512]{3,1,2,0:T(8,128)} copy(f32[103,8,2,512]{3,2,1,0:T(2,128)S(1)} %bitcast.153) | data formatting | bytes 6750208
  27.4 1.0 %maximum_convert_fusion = f32[822,2,514]{2,0,1:T(8,128)S(1)} fusion(bf16[822,2,1]{2,0,1:T(8,128)(2,1)S(1)} %collective-permute-done.1, bf16[822,2,512]{2,0,1:T(8,128)(2,1)S(1)} %copy-done.3, bf16[822,2,1]{2,0,1:T(8,128)(2,1)S(1)} %collective-permute-done), kind=kLoop, calls=%fused_computation.2 | loop fusion | flops 5070096 | bytes 5070096 | tf_op jit(solution)/shard_map/convert_element_type | solution.py:56
  28.4 1.9 %fusion.10 = bf16[256,512]{0,1:T(8,128)(2,1)S(1)} fusion(bf16[256,822]{0,1:T(8,128)(2,1)S(1)} %copy-done.13, f32[822,2,514]{2,0,1:T(8,128)S(1)} %maximum_convert_fusion, f32[822]{0:T(1024)S(1)} %get-tuple-element.9, f32[822]{0:T(1024)S(1)} %get-tuple-element.10, f32[822]{0:T(1024)S(1)} %get-tuple-element.3), kind=kOutput, calls=%fused_computation.27 | convolution fusion | flops 218138624 | bytes 5758976 | tf_op jit(solution)/shard_map/dot_general | solution.py:65
  30.3 3.9 %collective-permute-start.2 = (bf16[256,512]{0,1:T(8,128)(2,1)S(1)}, bf16[256,512]{0,1:T(8,128)(2,1)S(1)}, u32[]{:S(2)}, u32[]{:S(2)}) collective-permute-start(bf16[256,512]{0,1:T(8,128)(2,1)S(1)} %fusion.10), channel_id=1, source_target_pairs={{0,4},{4,8},{8,12},{12,16},{16,20},{20,24},{24,28},{1,5},{5,9},{9,... | collective-permute-start | bytes 786440 | tf_op jit(solution)/shard_map/ppermute | solution.py:70
  34.2 1.9 %fusion.11 = bf16[256,512]{0,1:T(8,128)(2,1)S(1)} fusion(bf16[256,822]{0,1:T(8,128)(2,1)S(1)} %copy-done.13, f32[822,2,514]{2,0,1:T(8,128)S(1)} %maximum_convert_fusion, f32[822]{0:T(1024)S(1)} %get-tuple-element.4, f32[822]{0:T(1024)S(1)} %get-tuple-element.5, f32[822]{0:T(1024)S(1)} %get-tuple-element.2), kind=kOutput, calls=%fused_computation.28 | convolution fusion | flops 218138624 | bytes 5758976 | tf_op jit(solution)/shard_map/dot_general | solution.py:65
  36.1 1.5 %collective-permute-start.3 = (bf16[256,512]{0,1:T(8,128)(2,1)S(1)}, bf16[256,512]{0,1:T(8,128)(2,1)S(1)}, u32[]{:S(2)}, u32[]{:S(2)}) collective-permute-start(bf16[256,512]{0,1:T(8,128)(2,1)S(1)} %fusion.11), channel_id=1, source_target_pairs={{4,0},{8,4},{12,8},{16,12},{20,16},{24,20},{28,24},{5,1},{9,5},{13... | collective-permute-start | bytes 786440 | tf_op jit(solution)/shard_map/ppermute | solution.py:71
  37.5 1.7 %collective-permute-done.2 = bf16[256,512]{0,1:T(8,128)(2,1)S(1)} collective-permute-done((bf16[256,512]{0,1:T(8,128)(2,1)S(1)}, bf16[256,512]{0,1:T(8,128)(2,1)S(1)}, u32[]{:S(2)}, u32[]{:S(2)}) %collective-permute-start.2) | collective-permute-done | bytes 262176 | tf_op jit(solution)/shard_map/ppermute | solution.py:70
  39.2 3.0 %fusion.6 = f32[256,512]{0,1:T(8,128)S(1)} fusion(f32[256,512]{0,1:T(8,128)S(1)} %fusion.30, bf16[256,822]{0,1:T(8,128)(2,1)S(1)} %copy-done.13, f32[822,2,514]{2,0,1:T(8,128)S(1)} %maximum_convert_fusion, f32[822]{0:T(1024)S(1)} %get-tuple-element.4, f32[822]{0:T(1024)S(1)} %get-tuple-element.5, f32[822]{0:T(1024)S(1)} %get-tuple-element.2, ...), kind=kOutput, calls=%fused_computation.21 | convolution fusion | flops 220925952 | bytes 11882496 | tf_op jit(solution)/shard_map/dot_general | solution.py:65
  43.5 6.6 %all-to-all-start.1 = ((bf16[8,96,128]{2,1,0:T(8,128)(2,1)}), bf16[8,96,128]{2,1,0:T(8,128)(2,1)S(1)}, u32[]{:S(2)}, u32[]{:S(2)}) async-start(bf16[8,96,128]{2,1,0:T(8,128)(2,1)} %broadcast_in_dim.7), calls=%async_computation.1 | async-start | bytes 393216 | tf_op jit(solution)/shard_map/all_to_all | solution.py:101
  50.1 8.9 %fusion.4 = f32[256,512]{0,1:T(8,128)S(1)} fusion(f32[256,512]{0,1:T(8,128)} %fusion.29, bf16[256,822]{0,1:T(8,128)(2,1)S(1)} %copy-done.13, f32[822,2,514]{2,0,1:T(8,128)} %copy-done.4, f32[822]{0:T(1024)S(1)} %get-tuple-element.9, f32[822]{0:T(1024)S(1)} %get-tuple-element.10, f32[822]{0:T(1024)S(1)} %get-tuple-element.3, f32[822]{0:T(1024)S(1)} %get-tuple-element.6, ...), kind=kOutput, calls=%fused_computation.18 | convolution fusion | flops 220925952 | bytes 11876624 | tf_op jit(solution)/shard_map/dot_general | solution.py:65
  59.2 1.6 %fusion.17 = f32[256,1024]{0,1:T(8,128)S(1)} fusion(bf16[256,822]{0,1:T(8,128)(2,1)} %param.20, bf16[96,822]{1,0:T(8,128)(2,1)S(1)} %copy-done.5, bf16[12,8,8,128]{3,2,1,0:T(8,128)(2,1)S(1)} %bitcast.154), kind=kOutput, calls=%fused_computation.34 | convolution fusion | flops 90759168 | bytes 1823872 | tf_op jit(solution)/shard_map/dot_general | solution.py:104
  60.8 4.0 %fusion = bf16[822,1024]{1,0:T(8,128)(2,1)} fusion(f32[822,1024]{1,0:T(8,128)} %bitcast.152, bf16[822,256]{1,0:T(8,128)(2,1)S(1)} %copy-done, f32[256,1024]{0,1:T(8,128)S(1)} %fusion.17, f32[256,512]{0,1:T(8,128)S(1)} %fusion.4, f32[256,512]{0,1:T(8,128)S(1)} %fusion.6, f32[256]{0:T(256)S(1)} %copy-done.12), kind=kOutput, calls=%fused_computation.1 | convolution fusion | flops 435793920 | bytes 7569408 | tf_op jit(solution)/shard_map/dot_general | solution.py:106
  64.8 5.1 %reshape.45 = bf16[822,2,512]{2,1,0:T(2,128)(2,1)} reshape(bf16[822,1024]{1,0:T(8,128)(2,1)} %fusion) | data formatting | bytes 3366912 | tf_op jit(solution)/shard_map/reshape | solution.py:109
  (50 shorter events, 2.5 us)
Async XLA Ops:
  0.6 60.2 %copy-start = (bf16[822,256]{1,0:T(8,128)(2,1)S(1)}, bf16[822,256]{1,0:T(8,128)(2,1)}, u32[]{:S(2)}) copy-start(bf16[822,256]{1,0:T(8,128)(2,1)} %param.22) | copy-start | bytes 1262596
  2.4 1.2 %copy-start.2 = (bf16[822,2,512]{2,0,1:T(8,128)(2,1)}, bf16[822,2,512]{2,0,1:T(8,128)(2,1)S(1)}, u32[]{:S(2)}) copy-start(bf16[822,2,512]{2,0,1:T(8,128)(2,1)S(1)} %copy.67) | copy-start | bytes 5050372
  3.6 3.5 %copy-start.1 = (bf16[822,2,512]{2,1,0:T(2,128)(2,1)S(1)}, bf16[822,2,512]{2,1,0:T(2,128)(2,1)}, u32[]{:S(2)}) copy-start(bf16[822,2,512]{2,1,0:T(2,128)(2,1)} %param.16) | copy-start | bytes 5050372
  4.7 4.8 %copy-start.11 = (s32[1,1,8,4]{2,3,1,0:T(4,128)S(1)}, s32[1,1,8,4]{2,3,1,0:T(4,128)}, u32[]{:S(2)}) copy-start(s32[1,1,8,4]{2,3,1,0:T(4,128)} %param.31) | copy-start | bytes 388
  4.7 22.7 %collective-permute-start = (bf16[822,2,1]{2,0,1:T(8,128)(2,1)}, bf16[822,2,1]{2,0,1:T(8,128)(2,1)S(1)}, u32[]{:S(2)}, u32[]{:S(2)}) collective-permute-start(bf16[822,2,1]{2,0,1:T(8,128)(2,1)} %get-tuple-element.11), channel_id=1, source_target_pairs={{0,1},{1,2},{2,3},{3,0},{4,5},{5,6},{6,7},{7,4},{8,9},{9,10},{10,1... | collective-permute-start | bytes 9872 | tf_op jit(solution)/shard_map/ppermute | solution.py:17
  5.2 4.4 %copy-start.5 = (bf16[96,822]{1,0:T(8,128)(2,1)S(1)}, bf16[96,822]{1,0:T(8,128)(2,1)}, u32[]{:S(2)}) copy-start(bf16[96,822]{1,0:T(8,128)(2,1)} %param.23) | copy-start | bytes 473476
  5.2 22.2 %collective-permute-start.1 = (bf16[822,2,1]{2,0,1:T(8,128)(2,1)}, bf16[822,2,1]{2,0,1:T(8,128)(2,1)S(1)}, u32[]{:S(2)}, u32[]{:S(2)}) collective-permute-start(bf16[822,2,1]{2,0,1:T(8,128)(2,1)} %get-tuple-element.12), channel_id=1, source_target_pairs={{1,0},{2,1},{3,2},{0,3},{5,4},{6,5},{7,6},{4,7},{9,8},{10,9},{11,1... | collective-permute-start | bytes 9872 | tf_op jit(solution)/shard_map/ppermute | solution.py:18
  12.4 29.9 %all-to-all-start = ((bf16[8,96,128]{2,1,0:T(8,128)(2,1)}), bf16[8,96,128]{2,1,0:T(8,128)(2,1)S(1)}, u32[]{:S(2)}, u32[]{:S(2)}) async-start(bf16[8,96,128]{2,1,0:T(8,128)(2,1)} %copy.77), calls=%async_computation | async-start | bytes 393216 | tf_op jit(solution)/shard_map/all_to_all | solution.py:87
  19.0 2.0 %copy-start.3 = (bf16[822,2,512]{2,0,1:T(8,128)(2,1)S(1)}, bf16[822,2,512]{2,0,1:T(8,128)(2,1)}, u32[]{:S(2)}) copy-start(bf16[822,2,512]{2,0,1:T(8,128)(2,1)} %copy-done.2) | copy-start | bytes 5050372
  19.0 4.3 %copy-start.6 = (s32[96,1,128]{2,1,0:T(1,128)S(1)}, s32[96,1,128]{2,1,0:T(1,128)}, u32[]{:S(2)}) copy-start(s32[96,1,128]{2,1,0:T(1,128)} %param.25) | copy-start | bytes 147460
  19.0 4.4 %copy-start.7 = (bf16[256,96]{0,1:T(8,128)(2,1)S(1)}, bf16[256,96]{0,1:T(8,128)(2,1)}, u32[]{:S(2)}) copy-start(bf16[256,96]{0,1:T(8,128)(2,1)} %param.28) | copy-start | bytes 147460
  19.0 4.4 %copy-start.8 = (bf16[96,1,128]{2,0,1:T(8,128)(2,1)S(1)}, bf16[96,1,128]{2,0,1:T(8,128)(2,1)}, u32[]{:S(2)}) copy-start(bf16[96,1,128]{2,0,1:T(8,128)(2,1)} %param.26) | copy-start | bytes 73732
  19.0 4.6 %copy-start.10 = (f32[822,3,3]{0,2,1:T(4,128)S(1)}, f32[822,3,3]{0,2,1:T(4,128)}, u32[]{:S(2)}) copy-start(f32[822,3,3]{0,2,1:T(4,128)} %param.17) | copy-start | bytes 88780
  27.4 1.0 %copy-start.13 = (bf16[256,822]{0,1:T(8,128)(2,1)S(1)}, bf16[256,822]{0,1:T(8,128)(2,1)}, u32[]{:S(2)}) copy-start(bf16[256,822]{0,1:T(8,128)(2,1)} %param.19) | copy-start | bytes 1262596
  28.4 10.8 %copy-start.4 = (f32[822,2,514]{2,0,1:T(8,128)}, f32[822,2,514]{2,0,1:T(8,128)S(1)}, u32[]{:S(2)}) copy-start(f32[822,2,514]{2,0,1:T(8,128)S(1)} %maximum_convert_fusion) | copy-start | bytes 10140196
  30.3 8.9 %collective-permute-start.2 = (bf16[256,512]{0,1:T(8,128)(2,1)S(1)}, bf16[256,512]{0,1:T(8,128)(2,1)S(1)}, u32[]{:S(2)}, u32[]{:S(2)}) collective-permute-start(bf16[256,512]{0,1:T(8,128)(2,1)S(1)} %fusion.10), channel_id=1, source_target_pairs={{0,4},{4,8},{8,12},{12,16},{16,20},{20,24},{24,28},{1,5},{5,9},{9,... | collective-permute-start | bytes 786440 | tf_op jit(solution)/shard_map/ppermute | solution.py:70
  36.1 14.0 %collective-permute-start.3 = (bf16[256,512]{0,1:T(8,128)(2,1)S(1)}, bf16[256,512]{0,1:T(8,128)(2,1)S(1)}, u32[]{:S(2)}, u32[]{:S(2)}) collective-permute-start(bf16[256,512]{0,1:T(8,128)(2,1)S(1)} %fusion.11), channel_id=1, source_target_pairs={{4,0},{8,4},{12,8},{16,12},{20,16},{24,20},{28,24},{5,1},{9,5},{13... | collective-permute-start | bytes 786440 | tf_op jit(solution)/shard_map/ppermute | solution.py:71
  39.2 3.1 %copy-start.14 = (bf16[96,256]{1,0:T(8,128)(2,1)S(1)}, bf16[96,256]{1,0:T(8,128)(2,1)}, u32[]{:S(2)}) copy-start(bf16[96,256]{1,0:T(8,128)(2,1)} %param.30) | copy-start | bytes 147460
  39.2 3.1 %copy-start.15 = (bf16[256,96]{0,1:T(8,128)(2,1)S(1)}, bf16[256,96]{0,1:T(8,128)(2,1)}, u32[]{:S(2)}) copy-start(bf16[256,96]{0,1:T(8,128)(2,1)} %param.27) | copy-start | bytes 147460
  39.2 3.1 %copy-start.16 = (f32[96,1,128]{2,1,0:T(1,128)S(1)}, f32[96,1,128]{2,1,0:T(1,128)}, u32[]{:S(2)}) copy-start(f32[96,1,128]{2,1,0:T(1,128)} %param.24) | copy-start | bytes 147460
  39.2 3.1 %copy-start.17 = (f32[256]{0:T(256)S(1)}, f32[256]{0:T(256)}, u32[]{:S(2)}) copy-start(f32[256]{0:T(256)} %param.29) | copy-start | bytes 3076
  42.8 16.2 %copy-start.9 = (bf16[96,128]{1,0:T(8,128)(2,1)}, bf16[96,128]{1,0:T(8,128)(2,1)S(1)}, u32[]{:S(2)}) copy-start(bf16[96,128]{1,0:T(8,128)(2,1)S(1)} %fusion.19) | copy-start | bytes 73732
  43.5 15.5 %all-to-all-start.1 = ((bf16[8,96,128]{2,1,0:T(8,128)(2,1)}), bf16[8,96,128]{2,1,0:T(8,128)(2,1)S(1)}, u32[]{:S(2)}, u32[]{:S(2)}) async-start(bf16[8,96,128]{2,1,0:T(8,128)(2,1)} %broadcast_in_dim.7), calls=%async_computation.1 | async-start | bytes 393216 | tf_op jit(solution)/shard_map/all_to_all | solution.py:101
  59.0 1.8 %copy-start.12 = (f32[256]{0:T(256)S(1)}, f32[256]{0:T(256)}, u32[]{:S(2)}) copy-start(f32[256]{0:T(256)} %param.21) | copy-start | bytes 3076

commit v2 on v0

v2 whole, which is shorter than its diff:
```python
import jax
import jax.numpy as jnp
import numpy as np
from jax import lax
from jax.experimental import pallas as pl
from jax.experimental.pallas import tpu as pltpu
from jax.sharding import PartitionSpec as P

PIX = 128
MESH = pl.DeviceIdType.MESH
STEP = 32
SLOTS = 16
EDGES = tuple((db, dl) for db in (0, -1, 1) for dl in (-1, 1))


def dot(a, b, da=1, db=0):
    return lax.dot_general(a, b, (((da,), (db,)), ((), ())), preferred_element_type=jnp.float32)


def picker(lat_rows):
    pick = np.zeros((len(EDGES) * SLOTS, lat_rows * 2 * PIX), np.float32)
    for m, (db, dl) in enumerate(EDGES):
        for i in range(lat_rows):
            relative = i - lat_rows * db
            if -1 <= relative <= lat_rows:
                if dl == -1:
                    pick[m * SLOTS + relative + 1, i * 2 * PIX] = 1.0
                else:
                    pick[m * SLOTS + lat_rows + 2 + relative + 1, i * 2 * PIX + 2 * PIX - 1] = 1.0
    return pick


def kernel_body(
    state,
    taps,
    edge0,
    edge1,
    ws_t,
    wc_t,
    wa_t,
    bias,
    w_out,
    obs_op,
    observed,
    valid,
    dual_in,
    res_t,
    prev_t,
    dual_bias,
    dual_out_w,
    cover,
    pick,
    out,
    dual_new,
    xb,
    wide,
    rows,
    mix,
    pre,
    zbuf,
    share,
    arrived,
    gathered,
    back,
    through_t,
    hid,
    psend,
    precv,
    esend,
    erecv,
    load_sem,
    a_send,
    a_recv,
    g_send,
    g_recv,
    p_send,
    p_recv,
    e_send,
    e_recv,
):
    channels = ws_t.shape[0]
    lon_cols = xb.shape[1]
    per_row = lon_cols // PIX
    radiance = obs_op.shape[0]
    nb = lax.axis_size("band")
    nl = lax.axis_size("lon")
    nblocks = 2 * per_row
    b = lax.axis_index("band")
    l = lax.axis_index("lon")
    flat = state.reshape(2 * channels, lon_cols)
    load = pltpu.make_async_copy(flat, xb, load_sem.at[0])
    load.start()

    precv[...] = jnp.zeros_like(precv)
    erecv[...] = jnp.zeros_like(erecv)
    barrier = pltpu.get_barrier_semaphore()

    def greet(off, carry):
        pl.semaphore_signal(
            barrier, inc=1, device_id=(lax.rem(b + off, nb), l), device_id_type=MESH
        )
        return carry

    lax.fori_loop(1, nb, greet, 0)
    for db, dl in EDGES:

        @pl.when((b + db >= 0) & (b + db < nb))
        def _():
            pl.semaphore_signal(
                barrier, inc=1, device_id=(b + db, lax.rem(l + dl + nl, nl)), device_id_type=MESH
            )

    through_t[...] = dot(obs_op[...], wa_t[...]).astype(jnp.bfloat16)
    load.wait()

    whole = channels // STEP * STEP

    def chunks(body):
        def step(i, carry):
            body(pl.multiple_of(i * STEP, STEP), STEP)
            return carry

        lax.fori_loop(0, whole // STEP, step, 0)
        if channels > whole:
            body(whole, channels - whole)

    def split(c0, n):
        both = xb[pl.ds(2 * c0, 2 * n), :].astype(jnp.float32)
        for q in range(per_row):
            wide[q, pl.ds(2 * c0, 2 * n), :] = both[:, q * PIX : (q + 1) * PIX]
        for i in range(2):
            for q in range(per_row):
                rows[i, pl.ds(c0, n), q * PIX : (q + 1) * PIX] = wide[
                    q, pl.ds(2 * c0 + i, n, 2), :
                ].astype(jnp.bfloat16)

    chunks(split)
    for i in range(2):
        zbuf[:, i * lon_cols : (i + 1) * lon_cols] = dot(obs_op[...], rows[i]).astype(jnp.bfloat16)

    pl.semaphore_wait(
        barrier,
        nb - 1 + 2 + 2 * (b > 0).astype(jnp.int32) + 2 * (b < nb - 1).astype(jnp.int32),
    )

    def to_owner(off):
        d = lax.rem(b + off, nb)
        return pltpu.make_async_remote_copy(
            src_ref=share.at[d],
            dst_ref=arrived.at[off],
            send_sem=a_send.at[off],
            recv_sem=a_recv.at[off],
            device_id=(d, l),
            device_id_type=MESH,
        )

    def make_share(off):
        d = lax.rem(b + off, nb)
        total = jnp.zeros((radiance, PIX), jnp.float32)
        for k in range(nblocks):
            total = total + cover[k, d] * zbuf[:, k * PIX : (k + 1) * PIX].astype(jnp.float32)
        share[d] = total.astype(jnp.bfloat16)

    def send_share(off, carry):
        make_share(off)
        to_owner(off).start()
        return carry

    lax.fori_loop(1, nb, send_share, 0)
    make_share(0)

    lane = lax.broadcasted_iota(jnp.int32, (1, lon_cols), 1)

    def taps_of(targets):
        def body(c0, n):
            x = [rows[i, pl.ds(c0, n), :].astype(jnp.float32) for i in range(2)]
            tap = taps[pl.ds(c0, n), :]
            for t in targets:
                parts = []
                for e in range(3):
                    total = None
                    for i in range(2):
                        a = i - (t - 1) + 1
                        if 0 <= a < 3:
                            term = tap[:, 3 * a + e : 3 * a + e + 1] * x[i]
                            total = term if total is None else total + term
                    parts.append(total)
                west = jnp.where(lane == 0, 0.0, pltpu.roll(parts[0], 1, 1))
                east = jnp.where(lane == lon_cols - 1, 0.0, pltpu.roll(parts[2], lon_cols - 1, 1))
                mix[t, pl.ds(c0, n), :] = (parts[1] + west + east).astype(jnp.bfloat16)

        return body

    chunks(taps_of((0, 3)))

    def to_neighbour(which):
        return pltpu.make_async_remote_copy(
            src_ref=psend.at[which],
            dst_ref=precv.at[which],
            send_sem=p_send.at[which],
            recv_sem=p_recv.at[which],
            device_id=(b - 1 if which == 0 else b + 1, l),
            device_id_type=MESH,
        )

    reaches = (b > 0, b < nb - 1)
    for which in range(2):
        psend[which] = dot(wc_t[...], mix[3 * which], 0, 0).astype(jnp.bfloat16)

        @pl.when(reaches[which])
        def _():
            to_neighbour(which).start()

    elane = lax.broadcasted_iota(jnp.int32, (1, PIX), 1)
    ends = []
    for i in range(2):
        initial = rows[i, :, 0:PIX].astype(jnp.float32)[:, 0:1]
        last = rows[i, :, lon_cols - PIX : lon_cols].astype(jnp.float32)[:, PIX - 1 : PIX]
        ends.append(jnp.where(elane < 4, last, initial))
    edge = (ends[0] * edge0[...] + ends[1] * edge1[...]).astype(jnp.bfloat16)
    esend[...] = dot(edge, wc_t[...], 0, 0)[0:SLOTS].astype(jnp.bfloat16)

    def to_edge(m):
        db, dl = EDGES[m]
        return pltpu.make_async_remote_copy(
            src_ref=esend,
            dst_ref=erecv.at[pl.ds(m * SLOTS, SLOTS)],
            send_sem=e_send.at[m],
            recv_sem=e_recv.at[m],
            device_id=(b - db, lax.rem(l - dl + nl, nl)),
            device_id_type=MESH,
        )

    for m, (db, dl) in enumerate(EDGES):

        @pl.when((b - db >= 0) & (b - db < nb))
        def _():
            to_edge(m).start()

    def take_share(off, total):
        to_owner(off).wait_recv()
        return total + arrived[off].astype(jnp.float32)

    evolved = lax.fori_loop(1, nb, take_share, share[b].astype(jnp.float32))
    departure = jnp.where(valid[...] == 1, evolved - observed[...], 0.0).astype(jnp.bfloat16)
    pre_dual = dot(res_t[...], departure, 0, 0) + dot(prev_t[...], dual_in[...], 0, 0)
    dual_hidden = jax.nn.gelu(pre_dual + dual_bias[...]).astype(jnp.bfloat16)
    updated = dual_in[...].astype(jnp.float32) + dot(dual_out_w[...], dual_hidden)
    gathered[0] = updated.astype(jnp.bfloat16)
    dual_new[...] = updated.astype(jnp.bfloat16)

    def to_all(off):
        return pltpu.make_async_remote_copy(
            src_ref=gathered.at[0],
            dst_ref=gathered.at[off],
            send_sem=g_send.at[off],
            recv_sem=g_recv.at[off],
            device_id=(lax.rem(b + off, nb), l),
            device_id_type=MESH,
        )

    def send_dual(off, carry):
        to_all(off).start()
        return carry

    lax.fori_loop(1, nb, send_dual, 0)

    chunks(taps_of((1, 2)))
    for i in range(2):
        pre[i] = dot(ws_t[...], rows[i], 0, 0) + dot(wc_t[...], mix[1 + i], 0, 0) + bias[...]

    def landed(off, carry):
        to_all(off).wait_recv()
        return carry

    lax.fori_loop(1, nb, landed, 0)
    for r in range(0, radiance, 16):

        def gather_in(off, totals):
            d = lax.rem(b - off + nb, nb)
            block = gathered[off, r : r + 16, :].astype(jnp.float32)
            return tuple(totals[k] + cover[k, d] * block for k in range(nblocks))

        zero = jnp.zeros((16, PIX), jnp.float32)
        totals = lax.fori_loop(0, nb, gather_in, (zero,) * nblocks, unroll=nb <= 8)
        for k in range(nblocks):
            back[r : r + 16, k * PIX : (k + 1) * PIX] = totals[k].astype(jnp.bfloat16)

    for m, (db, dl) in enumerate(EDGES):

        @pl.when((b + db >= 0) & (b + db < nb))
        def _():
            to_edge(m).wait_recv()

    fix = dot(erecv[...], pick[...], 0, 0)
    for i in range(2):
        pre[i] = pre[i] + dot(
            through_t[...], back[:, i * lon_cols : (i + 1) * lon_cols], 0, 0
        )
        pre[i, :, 0:PIX] = pre[i, :, 0:PIX] + fix[:, 2 * i * PIX : (2 * i + 1) * PIX]
        pre[i, :, lon_cols - PIX :] = (
            pre[i, :, lon_cols - PIX :] + fix[:, (2 * i + 1) * PIX : (2 * i + 2) * PIX]
        )
    for i in range(2):
        came = 1 - i

        @pl.when(reaches[i])
        def _():
            to_neighbour(came).wait_recv()

        for q in range(per_row):
            cols = slice(q * PIX, (q + 1) * PIX)
            hid[:, cols] = jax.nn.gelu(
                pre[i, :, cols] + precv[came, :, cols].astype(jnp.float32)
            ).astype(jnp.bfloat16)
        for q in range(per_row):
            cols = slice(q * PIX, (q + 1) * PIX)
            place = pl.ds(i, channels, 2)
            wide[q, place, :] = wide[q, place, :] + dot(w_out[...], hid[:, cols])

    def pack(c0, n):
        for q in range(per_row):
            xb[pl.ds(2 * c0, 2 * n), q * PIX : (q + 1) * PIX] = wide[
                q, pl.ds(2 * c0, 2 * n), :
            ].astype(jnp.bfloat16)

    chunks(pack)
    store = pltpu.make_async_copy(xb, out.reshape(2 * channels, lon_cols), load_sem.at[0])
    store.start()

    def sent(off, carry):
        to_owner(off).wait_send()
        to_all(off).wait_send()
        return carry

    lax.fori_loop(1, nb, sent, 0)
    for which in range(2):

        @pl.when(reaches[which])
        def _():
            to_neighbour(which).wait_send()

    for m, (db, dl) in enumerate(EDGES):

        @pl.when((b - db >= 0) & (b - db < nb))
        def _():
            to_edge(m).wait_send()

    store.wait()


def on_device(
    state,
    kernel,
    w_state,
    w_conv,
    w_adj,
    bias_in,
    w_out,
    obs_op,
    observations,
    obs_mask,
    dual_in,
    dual_res,
    dual_prev,
    dual_bias,
    dual_out_w,
    footprint,
):
    channels, lat_rows, lon_cols = state.shape
    assert lat_rows == 2
    radiance = obs_op.shape[0]
    hidden = w_state.shape[0]
    nb = lax.axis_size("band")
    nblocks = lat_rows * lon_cols // PIX
    routes = footprint.reshape(nblocks, footprint.shape[-1])
    targets = jnp.arange(nb, dtype=jnp.int32)
    member = (routes[:, :, None] == targets[None, None, :]).astype(jnp.float32)
    cover = jnp.sum(member, axis=1)
    taps = kernel.reshape(channels, 9)
    none = jnp.zeros((channels,), jnp.float32)
    west, east = ([kernel[:, a, e] for a in range(3)] for e in (0, 2))
    on0 = [west[2], west[1], west[0], none, east[2], east[1], east[0], none]
    on1 = [none, west[2], west[1], west[0], none, east[2], east[1], east[0]]
    edge0, edge1 = (
        jnp.pad(jnp.stack(cols, axis=1), ((0, 0), (0, PIX - len(cols)))) for cols in (on0, on1)
    )
    pick = jnp.asarray(picker(lat_rows), jnp.bfloat16)
    vmem = pl.BlockSpec(memory_space=pltpu.VMEM)
    anywhere = pl.BlockSpec(memory_space=pl.ANY)
    smem = pl.BlockSpec(memory_space=pltpu.SMEM)
    dma = pltpu.SemaphoreType.DMA
    bf16, f32 = jnp.bfloat16, jnp.float32
    state_out, dual_new = pl.pallas_call(
        kernel_body,
        out_shape=(
            jax.ShapeDtypeStruct(state.shape, bf16),
            jax.ShapeDtypeStruct((radiance, PIX), bf16),
        ),
        in_specs=[anywhere] + [vmem] * 16 + [smem, vmem],
        out_specs=(anywhere, vmem),
        scratch_shapes=[
            pltpu.VMEM((2 * channels, lon_cols), bf16),
            pltpu.VMEM((lon_cols // PIX, 2 * channels, PIX), f32),
            pltpu.VMEM((2, channels, lon_cols), bf16),
            pltpu.VMEM((4, channels, lon_cols), bf16),
            pltpu.VMEM((2, hidden, lon_cols), f32),
            pltpu.VMEM((radiance, nblocks * PIX), bf16),
            pltpu.VMEM((nb, radiance, PIX), bf16),
            pltpu.VMEM((nb, radiance, PIX), bf16),
            pltpu.VMEM((nb, radiance, PIX), bf16),
            pltpu.VMEM((radiance, nblocks * PIX), bf16),
            pltpu.VMEM((radiance, hidden), bf16),
            pltpu.VMEM((hidden, lon_cols), bf16),
            pltpu.VMEM((2, hidden, lon_cols), bf16),
            pltpu.VMEM((2, hidden, lon_cols), bf16),
            pltpu.VMEM((SLOTS, hidden), bf16),
            pltpu.VMEM((len(EDGES) * SLOTS, hidden), bf16),
            dma((1,)),
            dma((nb,)),
            dma((nb,)),
            dma((nb,)),
            dma((nb,)),
            dma((2,)),
            dma((2,)),
            dma((len(EDGES),)),
            dma((len(EDGES),)),
        ],
        compiler_params=pltpu.CompilerParams(
            collective_id=0, has_side_effects=True, vmem_limit_bytes=40 << 20
        ),
    )(
        state,
        taps,
        edge0,
        edge1,
        w_state.T,
        w_conv.T,
        w_adj.T,
        bias_in[:, None],
        w_out,
        obs_op,
        observations.reshape(radiance, PIX),
        obs_mask.reshape(radiance, PIX),
        dual_in.reshape(radiance, PIX),
        dual_res.T,
        dual_prev.T,
        dual_bias[:, None],
        dual_out_w,
        cover,
        pick,
    )
    return (state_out, dual_new.reshape(radiance, 1, PIX))


def solution(mesh):
    in_specs = (
        P(None, "band", "lon"),
        P(),
        P(),
        P(),
        P(),
        P(),
        P(),
        P(),
        P(None, "band", "lon"),
        P(None, "band", "lon"),
        P(None, "band", "lon"),
        P(),
        P(),
        P(),
        P(),
        P("band", "lon", None, None),
    )
    out_specs = (P(None, "band", "lon"), P(None, "band", "lon"))
    return jax.shard_map(
        on_device, mesh=mesh, in_specs=in_specs, out_specs=out_specs, check_vma=False
    )
```

time: 124 us -> 52.8 us (0.43)
  the two profiles are of different devices: /device:TPU:0 before, /device:TPU:5 now
where the time goes in v2:
time: 52.8 us; the launch traced here: 51.9 us
  Pallas kernels  32.1 us (61%)
  local copies, waits for them, and re-layouts  17.7 us (34%)
  other arithmetic  1.35 us (3%)
  between operations  0.79 us (1%)
    pallas_call x1, Pallas kernels, on_device(): pl.pallas_call(kernel_body, out_shape=(jax.ShapeDtypeStruct(state.shape,...  32.1 us
    unnamed x30, local copies, waits for them, and re-layouts  8.72 us
    another operation x5, local copies, waits for them, and re-layouts, on_device(): jnp.stack(cols, axis=1)  4.17 us
    pad x2, local copies, waits for them, and re-layouts, on_device(): jnp.pad(jnp.stack(cols, axis=1), ((0, 0), (0, PIX - len(cols))))  2.07 us
    reduce_sum x1, other arithmetic, on_device(): cover = jnp.sum(member, axis=1)  1.35 us

profile of v2, /device:TPU:5, one launch (start us, length us, event | category | flops | bytes accessed | tf_op | source)
XLA Modules:
  0.0 51.9 jit_solution(381507980655711714)
XLA Ops:
  0.6 1.4 %convert_reduce_fusion.cover = f32[8,8]{1,0:T(8,128)} fusion(s32[8,4]{0,1:T(4,128)} %bitcast.35), kind=kLoop, calls=%fused_computation | loop fusion | flops 704 | bytes 384 | tf_op jit(solution)/shard_map/reduce_sum | solution.py:379
  2.0 0.8 %slice_bitcast_fusion = (f32[822,1]{0,1:T(1,128)S(1)}, f32[822,1]{0,1:T(1,128)S(1)}, f32[822,1]{0,1:T(1,128)S(1)}, f32[822,1]{0,1:T(1,128)S(1)}, f32[822,1]{0,1:T(1,128)S(1)}, /*index=5*/f32[822,1]{0,1:T(1,128)S(1)}) fusion(f32[822,3,3]{0,2,1:T(4,128)} %param.18), kind=kLoop, calls=%fused_computation.2 | loop fusion | bytes 39456 | tf_op jit(solution)/shard_map/stack;squeeze | solution.py:386
  2.8 0.7 %stack.7 = f32[822,8]{0,1:T(8,128)} concatenate(f32[822,1]{0,1:T(1,128)S(1)} %broadcast.7, f32[822,1]{0,1:T(1,128)S(1)} %get-tuple-element.10, f32[822,1]{0,1:T(1,128)S(1)} %get-tuple-element.9, f32[822,1]{0,1:T(1,128)S(1)} %get-tuple-element.8, f32[822,1]{0,1:T(1,128)S(1)} %broadcast.7, f32[822,1]{0,1:T(1,128)S(1)} %get-tuple-element.7, f32[822,1]{0,1:T(1,128)S(1)} %get-tuple-element.11, ...), dimensions={1} | concatenate | bytes 52608 | tf_op jit(solution)/shard_map/stack | solution.py:386
  3.5 0.1 stack.6
  3.5 0.8 %reshape.20 = f32[822,9]{0,1:T(8,128)S(1)} reshape(f32[822,3,3]{0,2,1:T(4,128)} %param.18) | data formatting | bytes 59184 | tf_op jit(solution)/shard_map/reshape | solution.py:380
  4.4 0.0 copy-start.6
  4.4 1.0 %copy.46.bias = f32[256,1]{1,0:T(8,128)S(1)} copy(f32[256,1]{0,1:T(1,128)} %bitcast.36) | data formatting | bytes 2048 | tf_op jit(solution)/shard_map/broadcast_in_dim | solution.py:440
  5.4 0.8 %copy.47.dual_bias = f32[256,1]{1,0:T(8,128)S(1)} copy(f32[256,1]{0,1:T(1,128)} %bitcast.37) | data formatting | bytes 2048 | tf_op jit(solution)/shard_map/broadcast_in_dim | solution.py:448
  6.2 0.2 copy.45.taps
  6.4 0.9 %copy.43 = f32[822,8]{1,0:T(8,128)} copy(f32[822,8]{0,1:T(8,128)S(1)} %stack.6) | data formatting | bytes 52608 | tf_op jit(solution)/shard_map/stack | solution.py:386
  7.3 1.0 %pad.7.edge0 = f32[822,128]{1,0:T(8,128)S(1)} pad(f32[822,8]{1,0:T(8,128)} %copy.43, f32[]{:T(128)} %constant.2.clone.1), padding=0_0x0_120 | pad | bytes 447172 | tf_op jit(solution)/shard_map/jit(_pad)/pad | solution.py:386
  8.4 1.7 %copy.44 = f32[822,8]{1,0:T(8,128)} copy(f32[822,8]{0,1:T(8,128)} %stack.7) | data formatting | bytes 52608 | tf_op jit(solution)/shard_map/stack | solution.py:386
  10.1 1.0 %pad.8.edge1 = f32[822,128]{1,0:T(8,128)S(1)} pad(f32[822,8]{1,0:T(8,128)} %copy.44, f32[]{:T(128)} %constant.2.clone.1), padding=0_0x0_120 | pad | bytes 447172 | tf_op jit(solution)/shard_map/jit(_pad)/pad | solution.py:386
  11.2 1.0 %copy-done.2 = bf16[256,822]{0,1:T(8,128)(2,1)S(1)} copy-done((bf16[256,822]{0,1:T(8,128)(2,1)S(1)}, bf16[256,822]{0,1:T(8,128)(2,1)}, u32[]{:S(2)}) %copy-start.2) | copy-done | bytes 420888
  12.2 1.0 %copy-done.3 = bf16[256,822]{0,1:T(8,128)(2,1)S(1)} copy-done((bf16[256,822]{0,1:T(8,128)(2,1)S(1)}, bf16[256,822]{0,1:T(8,128)(2,1)}, u32[]{:S(2)}) %copy-start.3) | copy-done | bytes 420888
  13.2 1.0 %copy-done.4 = bf16[822,256]{1,0:T(8,128)(2,1)S(1)} copy-done((bf16[822,256]{1,0:T(8,128)(2,1)S(1)}, bf16[822,256]{1,0:T(8,128)(2,1)}, u32[]{:S(2)}) %copy-start.4) | copy-done | bytes 420888
  14.2 0.8 %copy-done.8 = s32[96,1,128]{2,1,0:T(1,128)S(1)} copy-done((s32[96,1,128]{2,1,0:T(1,128)S(1)}, s32[96,1,128]{2,1,0:T(1,128)}, u32[]{:S(2)}) %copy-start.8) | copy-done | bytes 49176
  15.0 0.8 %copy-done.9 = bf16[256,96]{0,1:T(8,128)(2,1)S(1)} copy-done((bf16[256,96]{0,1:T(8,128)(2,1)S(1)}, bf16[256,96]{0,1:T(8,128)(2,1)}, u32[]{:S(2)}) %copy-start.9) | copy-done | bytes 49176
  15.8 0.8 %copy-done.10 = bf16[256,96]{0,1:T(8,128)(2,1)S(1)} copy-done((bf16[256,96]{0,1:T(8,128)(2,1)S(1)}, bf16[256,96]{0,1:T(8,128)(2,1)}, u32[]{:S(2)}) %copy-start.10) | copy-done | bytes 49176
  16.6 0.8 %copy-done.11 = bf16[96,256]{1,0:T(8,128)(2,1)S(1)} copy-done((bf16[96,256]{1,0:T(8,128)(2,1)S(1)}, bf16[96,256]{1,0:T(8,128)(2,1)}, u32[]{:S(2)}) %copy-start.11) | copy-done | bytes 49176
  17.4 0.7 %copy-done.13 = f32[8,8]{1,0:T(8,128)S(1)} copy-done((f32[8,8]{1,0:T(8,128)S(1)}, f32[8,8]{1,0:T(8,128)}, u32[]{:S(2)}) %copy-start.13) | copy-done | bytes 280
  18.1 32.1 %shard_map.176 = (bf16[822,2,512]{2,1,0:T(2,128)(2,1)S(1)}, bf16[96,128]{1,0:T(8,128)(2,1)S(1)}) custom-call(bf16[822,2,512]{2,1,0:T(2,128)(2,1)S(1)} %copy-done, f32[822,9]{1,0:T(8,128)S(1)} %copy.45.taps, f32[822,128]{1,0:T(8,128)S(1)} %pad.7.edge0, f32[822,128]{1,0:T(8,128)S(1)} %pad.8.edge1, bf16[822,256]{1,0:T(8,128)(2,1)S(1)} %bitcast.26, ...), custom_call_target="tpu_custom_call" | custom-call | tf_op jit(solution)/shard_map/pallas_call | solution.py:394
  50.2 1.2 %copy.50 = bf16[822,2,512]{2,1,0:T(2,128)(2,1)} copy(bf16[822,2,512]{2,1,0:T(2,128)(2,1)S(1)} %get-tuple-element.14) | data formatting | bytes 3366912
  51.3 0.6 %copy.51 = bf16[96,1,128]{2,0,1:T(8,128)(2,1)} copy(bf16[96,1,128]{2,0,1:T(8,128)(2,1)S(1)} %bitcast.34) | data formatting | bytes 49152
  (20 shorter events, 0.1 us)
Async XLA Ops:
  4.3 6.8 %copy-start = (bf16[822,2,512]{2,1,0:T(2,128)(2,1)S(1)}, bf16[822,2,512]{2,1,0:T(2,128)(2,1)}, u32[]{:S(2)}) copy-start(bf16[822,2,512]{2,1,0:T(2,128)(2,1)} %state.1) | copy-start | bytes 5050372
  4.3 6.8 %copy-start.1 = (bf16[256,822]{0,1:T(8,128)(2,1)S(1)}, bf16[256,822]{0,1:T(8,128)(2,1)}, u32[]{:S(2)}) copy-start(bf16[256,822]{0,1:T(8,128)(2,1)} %param.19) | copy-start | bytes 1262596
  4.4 6.8 %copy-start.5 = (bf16[96,822]{1,0:T(8,128)(2,1)S(1)}, bf16[96,822]{1,0:T(8,128)(2,1)}, u32[]{:S(2)}) copy-start(bf16[96,822]{1,0:T(8,128)(2,1)} %obs_op.1) | copy-start | bytes 473476
  4.4 6.8 %copy-start.6 = (bf16[96,512]{1,0:T(8,128)(2,1)S(1)}, bf16[96,512]{1,0:T(8,128)(2,1)}, u32[]{:S(2)}) copy-start(bf16[96,512]{1,0:T(8,128)(2,1)} %constant.3.clone.pick) | copy-start | bytes 294916
  4.4 6.8 %copy-start.7 = (f32[96,1,128]{2,1,0:T(1,128)S(1)}, f32[96,1,128]{2,1,0:T(1,128)}, u32[]{:S(2)}) copy-start(f32[96,1,128]{2,1,0:T(1,128)} %param.25) | copy-start | bytes 147460
  4.4 6.8 %copy-start.12 = (bf16[96,1,128]{2,0,1:T(8,128)(2,1)S(1)}, bf16[96,1,128]{2,0,1:T(8,128)(2,1)}, u32[]{:S(2)}) copy-start(bf16[96,1,128]{2,0,1:T(8,128)(2,1)} %param.27) | copy-start | bytes 73732
  11.2 1.0 %copy-start.2 = (bf16[256,822]{0,1:T(8,128)(2,1)S(1)}, bf16[256,822]{0,1:T(8,128)(2,1)}, u32[]{:S(2)}) copy-start(bf16[256,822]{0,1:T(8,128)(2,1)} %param.20) | copy-start | bytes 1262596
  12.2 1.0 %copy-start.3 = (bf16[256,822]{0,1:T(8,128)(2,1)S(1)}, bf16[256,822]{0,1:T(8,128)(2,1)}, u32[]{:S(2)}) copy-start(bf16[256,822]{0,1:T(8,128)(2,1)} %param.21) | copy-start | bytes 1262596
  13.2 1.0 %copy-start.4 = (bf16[822,256]{1,0:T(8,128)(2,1)S(1)}, bf16[822,256]{1,0:T(8,128)(2,1)}, u32[]{:S(2)}) copy-start(bf16[822,256]{1,0:T(8,128)(2,1)} %w_out.1) | copy-start | bytes 1262596
  14.2 0.8 %copy-start.8 = (s32[96,1,128]{2,1,0:T(1,128)S(1)}, s32[96,1,128]{2,1,0:T(1,128)}, u32[]{:S(2)}) copy-start(s32[96,1,128]{2,1,0:T(1,128)} %param.26) | copy-start | bytes 147460
  15.0 0.8 %copy-start.9 = (bf16[256,96]{0,1:T(8,128)(2,1)S(1)}, bf16[256,96]{0,1:T(8,128)(2,1)}, u32[]{:S(2)}) copy-start(bf16[256,96]{0,1:T(8,128)(2,1)} %param.28) | copy-start | bytes 147460
  15.8 0.8 %copy-start.10 = (bf16[256,96]{0,1:T(8,128)(2,1)S(1)}, bf16[256,96]{0,1:T(8,128)(2,1)}, u32[]{:S(2)}) copy-start(bf16[256,96]{0,1:T(8,128)(2,1)} %param.29) | copy-start | bytes 147460
  16.6 0.8 %copy-start.11 = (bf16[96,256]{1,0:T(8,128)(2,1)S(1)}, bf16[96,256]{1,0:T(8,128)(2,1)}, u32[]{:S(2)}) copy-start(bf16[96,256]{1,0:T(8,128)(2,1)} %dual_out_w.1) | copy-start | bytes 147460
  17.4 0.7 %copy-start.13 = (f32[8,8]{1,0:T(8,128)S(1)}, f32[8,8]{1,0:T(8,128)}, u32[]{:S(2)}) copy-start(f32[8,8]{1,0:T(8,128)} %convert_reduce_fusion.cover) | copy-start | bytes 772

commit v3 on v2

--- a/solution.py
+++ b/solution.py
@@ -1,6 +1,5 @@
 import jax
 import jax.numpy as jnp
-import numpy as np
 from jax import lax
 from jax.experimental import pallas as pl
 from jax.experimental.pallas import tpu as pltpu
@@ -17,71 +16,80 @@
     return lax.dot_general(a, b, (((da,), (db,)), ((), ())), preferred_element_type=jnp.float32)
 
 
-def picker(lat_rows):
-    pick = np.zeros((len(EDGES) * SLOTS, lat_rows * 2 * PIX), np.float32)
+def picker(shape):
+    row = lax.broadcasted_iota(jnp.int32, shape, 0)
+    col = lax.broadcasted_iota(jnp.int32, shape, 1)
+    pick = jnp.zeros(shape, jnp.float32)
     for m, (db, dl) in enumerate(EDGES):
-        for i in range(lat_rows):
-            relative = i - lat_rows * db
-            if -1 <= relative <= lat_rows:
-                if dl == -1:
-                    pick[m * SLOTS + relative + 1, i * 2 * PIX] = 1.0
-                else:
-                    pick[m * SLOTS + lat_rows + 2 + relative + 1, i * 2 * PIX + 2 * PIX - 1] = 1.0
-    return pick
+        for i in range(2):
+            relative = i - 2 * db
+            if -1 <= relative <= 2:
+                at = m * SLOTS + relative + 1 + (0 if dl == -1 else 4)
+                to = i * 2 * PIX + (0 if dl == -1 else 2 * PIX - 1)
+                pick = jnp.where((row == at) & (col == to), 1.0, pick)
+    return pick.astype(jnp.bfloat16)
 
 
 def kernel_body(
     state,
-    taps,
-    edge0,
-    edge1,
-    ws_t,
-    wc_t,
-    wa_t,
-    bias,
-    w_out,
-    obs_op,
-    observed,
-    valid,
-    dual_in,
-    res_t,
-    prev_t,
-    dual_bias,
-    dual_out_w,
-    cover,
-    pick,
-    out,
-    dual_new,
-    xb,
-    wide,
-    rows,
-    mix,
-    pre,
-    zbuf,
-    share,
-    arrived,
-    gathered,
-    back,
-    through_t,
-    hid,
-    psend,
-    precv,
-    esend,
-    erecv,
-    load_sem,
-    a_send,
-    a_recv,
-    g_send,
-    g_recv,
-    p_send,
-    p_recv,
-    e_send,
-    e_recv,
+    *refs,
 ):
+    inputs, spot, (out, dual_new), refs = refs[:14], refs[14], refs[15:17], refs[17:]
+    held, refs = refs[:14], refs[14:]
+    (
+        kern,
+        ws_t,
+        wc_t,
+        wa_t,
+        bias,
+        w_out,
+        obs_op,
+        observed,
+        valid,
+        dual_in,
+        res_t,
+        prev_t,
+        dual_bias,
+        dual_out_w,
+    ) = held
+    (
+        cover,
+        kern_rows,
+        taps,
+        ws,
+        wc,
+        xb,
+        wide,
+        rows,
+        mix,
+        pre,
+        zbuf,
+        share,
+        arrived,
+        gathered,
+        back,
+        through_t,
+        hid,
+        psend,
+        precv,
+        esend,
+        erecv,
+        load_sem,
+        in_sem,
+        a_send,
+        a_recv,
+        g_send,
+        g_recv,
+        p_send,
+        p_recv,
+        e_send,
+        e_recv,
+    ) = refs
     channels = ws_t.shape[0]
     lon_cols = xb.shape[1]
     per_row = lon_cols // PIX
     radiance = obs_op.shape[0]
+    hidden = ws_t.shape[1]
     nb = lax.axis_size("band")
     nl = lax.axis_size("lon")
     nblocks = 2 * per_row
@@ -90,6 +98,10 @@
     flat = state.reshape(2 * channels, lon_cols)
     load = pltpu.make_async_copy(flat, xb, load_sem.at[0])
     load.start()
+    fetches = [pltpu.make_async_copy(x, y, in_sem.at[i]) for i, (x, y) in enumerate(zip(inputs, held))]
+    order = (6, 0, 2, 8, 7, 9, 10, 11, 12, 13, 1, 4, 3, 5)
+    for i in order:
+        fetches[i].start()
 
     precv[...] = jnp.zeros_like(precv)
     erecv[...] = jnp.zeros_like(erecv)
@@ -110,17 +122,27 @@
                 barrier, inc=1, device_id=(b + db, lax.rem(l + dl + nl, nl)), device_id_type=MESH
             )
 
-    through_t[...] = dot(obs_op[...], wa_t[...]).astype(jnp.bfloat16)
+    def covers(d, carry):
+        for k in range(nblocks):
+            count = jnp.int32(0)
+            for t in range(spot.shape[0]):
+                count = count + (spot[t, k] == d).astype(jnp.int32)
+            cover[k, d] = count.astype(jnp.float32)
+        return carry
+
+    lax.fori_loop(0, nb, covers, 0)
+    kern_rows[...] = jnp.zeros_like(kern_rows)
     load.wait()
+    fetches[6].wait()
 
     whole = channels // STEP * STEP
 
-    def chunks(body):
+    def chunks(body, size=STEP, unroll=1):
         def step(i, carry):
-            body(pl.multiple_of(i * STEP, STEP), STEP)
+            body(pl.multiple_of(i * size, size), size)
             return carry
 
-        lax.fori_loop(0, whole // STEP, step, 0)
+        lax.fori_loop(0, whole // size, step, 0, unroll=unroll)
         if channels > whole:
             body(whole, channels - whole)
 
@@ -169,7 +191,19 @@
     lax.fori_loop(1, nb, send_share, 0)
     make_share(0)
 
+    fetches[0].wait()
+    for a in range(3):
+        for e, place in ((0, 2 - a), (2, 6 - a), (1, 8 + a)):
+            kern_rows[place : place + 1, 0:channels] = kern[a, e : e + 1, :]
+    taps[...] = kern_rows[...].T
+    fetches[2].wait()
+    wc[...] = wc_t[...].T
+
     lane = lax.broadcasted_iota(jnp.int32, (1, lon_cols), 1)
+
+    at = {}
+    for a in range(3):
+        at[a, 0], at[a, 2], at[a, 1] = 2 - a, 6 - a, 8 + a
 
     def taps_of(targets):
         def body(c0, n):
@@ -182,7 +216,7 @@
                     for i in range(2):
                         a = i - (t - 1) + 1
                         if 0 <= a < 3:
-                            term = tap[:, 3 * a + e : 3 * a + e + 1] * x[i]
+                            term = tap[:, at[a, e] : at[a, e] + 1] * x[i]
                             total = term if total is None else total + term
                     parts.append(total)
                 west = jnp.where(lane == 0, 0.0, pltpu.roll(parts[0], 1, 1))
@@ -191,7 +225,7 @@
 
         return body
 
-    chunks(taps_of((0, 3)))
+    chunks(taps_of((0, 3)), 16)
 
     def to_neighbour(which):
         return pltpu.make_async_remote_copy(
@@ -205,7 +239,7 @@
 
     reaches = (b > 0, b < nb - 1)
     for which in range(2):
-        psend[which] = dot(wc_t[...], mix[3 * which], 0, 0).astype(jnp.bfloat16)
+        psend[which] = dot(wc[...], mix[3 * which]).astype(jnp.bfloat16)
 
         @pl.when(reaches[which])
         def _():
@@ -217,7 +251,8 @@
         initial = rows[i, :, 0:PIX].astype(jnp.float32)[:, 0:1]
         last = rows[i, :, lon_cols - PIX : lon_cols].astype(jnp.float32)[:, PIX - 1 : PIX]
         ends.append(jnp.where(elane < 4, last, initial))
-    edge = (ends[0] * edge0[...] + ends[1] * edge1[...]).astype(jnp.bfloat16)
+    edge0 = jnp.where(elane < 8, taps[0:channels, :], 0.0)
+    edge = (ends[0] * edge0 + ends[1] * pltpu.roll(edge0, 1, 1)).astype(jnp.bfloat16)
     esend[...] = dot(edge, wc_t[...], 0, 0)[0:SLOTS].astype(jnp.bfloat16)
 
     def to_edge(m):
@@ -241,10 +276,14 @@
         to_owner(off).wait_recv()
         return total + arrived[off].astype(jnp.float32)
 
+    for i in range(7, 14):
+        fetches[i].wait()
     evolved = lax.fori_loop(1, nb, take_share, share[b].astype(jnp.float32))
     departure = jnp.where(valid[...] == 1, evolved - observed[...], 0.0).astype(jnp.bfloat16)
     pre_dual = dot(res_t[...], departure, 0, 0) + dot(prev_t[...], dual_in[...], 0, 0)
-    dual_hidden = jax.nn.gelu(pre_dual + dual_bias[...]).astype(jnp.bfloat16)
+    dual_hidden = jax.nn.gelu(
+        pre_dual + jnp.broadcast_to(dual_bias[...], (PIX, dual_bias.shape[1])).T
+    ).astype(jnp.bfloat16)
     updated = dual_in[...].astype(jnp.float32) + dot(dual_out_w[...], dual_hidden)
     gathered[0] = updated.astype(jnp.bfloat16)
     dual_new[...] = updated.astype(jnp.bfloat16)
@@ -265,9 +304,31 @@
 
     lax.fori_loop(1, nb, send_dual, 0)
 
-    chunks(taps_of((1, 2)))
+    fetches[3].wait()
+    through_t[...] = dot(obs_op[...], wa_t[...]).astype(jnp.bfloat16)
+    fetches[1].wait()
+    ws[...] = ws_t[...].T
+    chunks(taps_of((1, 2)), 16)
+    fetches[4].wait()
+    bias_wide = jnp.broadcast_to(bias[...], (PIX, hidden)).T
     for i in range(2):
-        pre[i] = dot(ws_t[...], rows[i], 0, 0) + dot(wc_t[...], mix[1 + i], 0, 0) + bias[...]
+        part = dot(ws[...], rows[i]) + dot(wc[...], mix[1 + i])
+        for q in range(per_row):
+            pre[i, :, q * PIX : (q + 1) * PIX] = part[:, q * PIX : (q + 1) * PIX] + bias_wide
+
+    for m, (db, dl) in enumerate(EDGES):
+
+        @pl.when((b + db >= 0) & (b + db < nb))
+        def _():
+            to_edge(m).wait_recv()
+
+    pick = picker((len(EDGES) * SLOTS, 4 * PIX))
+    fix = dot(erecv[...], pick, 0, 0)
+    for i in range(2):
+        pre[i, :, 0:PIX] = pre[i, :, 0:PIX] + fix[:, 2 * i * PIX : (2 * i + 1) * PIX]
+        pre[i, :, lon_cols - PIX :] = (
+            pre[i, :, lon_cols - PIX :] + fix[:, (2 * i + 1) * PIX : (2 * i + 2) * PIX]
+        )
 
     def landed(off, carry):
         to_all(off).wait_recv()
@@ -286,21 +347,10 @@
         for k in range(nblocks):
             back[r : r + 16, k * PIX : (k + 1) * PIX] = totals[k].astype(jnp.bfloat16)
 
-    for m, (db, dl) in enumerate(EDGES):
-
-        @pl.when((b + db >= 0) & (b + db < nb))
-        def _():
-            to_edge(m).wait_recv()
-
-    fix = dot(erecv[...], pick[...], 0, 0)
+    through = through_t[...].T
     for i in range(2):
-        pre[i] = pre[i] + dot(
-            through_t[...], back[:, i * lon_cols : (i + 1) * lon_cols], 0, 0
-        )
-        pre[i, :, 0:PIX] = pre[i, :, 0:PIX] + fix[:, 2 * i * PIX : (2 * i + 1) * PIX]
-        pre[i, :, lon_cols - PIX :] = (
-            pre[i, :, lon_cols - PIX :] + fix[:, (2 * i + 1) * PIX : (2 * i + 2) * PIX]
-        )
+        pre[i] = pre[i] + dot(through, back[:, i * lon_cols : (i + 1) * lon_cols])
+    fetches[5].wait()
     for i in range(2):
         came = 1 - i
 
@@ -313,10 +363,13 @@
             hid[:, cols] = jax.nn.gelu(
                 pre[i, :, cols] + precv[came, :, cols].astype(jnp.float32)
             ).astype(jnp.bfloat16)
-        for q in range(per_row):
-            cols = slice(q * PIX, (q + 1) * PIX)
+        for q in range(0, per_row, 2):
+            added = dot(w_out[...], hid[:, q * PIX : (q + 2) * PIX])
             place = pl.ds(i, channels, 2)
-            wide[q, place, :] = wide[q, place, :] + dot(w_out[...], hid[:, cols])
+            for h in range(2):
+                wide[q + h, place, :] = (
+                    wide[q + h, place, :] + added[:, h * PIX : (h + 1) * PIX]
+                )
 
     def pack(c0, n):
         for q in range(per_row):
@@ -373,33 +426,45 @@
     hidden = w_state.shape[0]
     nb = lax.axis_size("band")
     nblocks = lat_rows * lon_cols // PIX
-    routes = footprint.reshape(nblocks, footprint.shape[-1])
-    targets = jnp.arange(nb, dtype=jnp.int32)
-    member = (routes[:, :, None] == targets[None, None, :]).astype(jnp.float32)
-    cover = jnp.sum(member, axis=1)
-    taps = kernel.reshape(channels, 9)
-    none = jnp.zeros((channels,), jnp.float32)
-    west, east = ([kernel[:, a, e] for a in range(3)] for e in (0, 2))
-    on0 = [west[2], west[1], west[0], none, east[2], east[1], east[0], none]
-    on1 = [none, west[2], west[1], west[0], none, east[2], east[1], east[0]]
-    edge0, edge1 = (
-        jnp.pad(jnp.stack(cols, axis=1), ((0, 0), (0, PIX - len(cols)))) for cols in (on0, on1)
-    )
-    pick = jnp.asarray(picker(lat_rows), jnp.bfloat16)
+    routes = footprint.reshape(nblocks, footprint.shape[-1]).T
     vmem = pl.BlockSpec(memory_space=pltpu.VMEM)
-    anywhere = pl.BlockSpec(memory_space=pl.ANY)
+    anywhere = pl.BlockSpec(memory_space=pltpu.HBM)
+    hbm = pl.BlockSpec(memory_space=pltpu.HBM)
     smem = pl.BlockSpec(memory_space=pltpu.SMEM)
     dma = pltpu.SemaphoreType.DMA
     bf16, f32 = jnp.bfloat16, jnp.float32
+    held = (
+        kernel.transpose(1, 2, 0),
+        w_state.T,
+        w_conv.T,
+        w_adj.T,
+        bias_in[None, :],
+        w_out,
+        obs_op,
+        observations.reshape(radiance, PIX),
+        obs_mask.reshape(radiance, PIX),
+        dual_in.reshape(radiance, PIX),
+        dual_res.T,
+        dual_prev.T,
+        dual_bias[None, :],
+        dual_out_w,
+    )
+    padded = -(-channels // PIX) * PIX
     state_out, dual_new = pl.pallas_call(
         kernel_body,
         out_shape=(
             jax.ShapeDtypeStruct(state.shape, bf16),
             jax.ShapeDtypeStruct((radiance, PIX), bf16),
         ),
-        in_specs=[anywhere] + [vmem] * 16 + [smem, vmem],
+        in_specs=[anywhere] + [hbm] * len(held) + [smem],
         out_specs=(anywhere, vmem),
-        scratch_shapes=[
+        scratch_shapes=[pltpu.VMEM(x.shape, x.dtype) for x in held]
+        + [
+            pltpu.SMEM((nblocks, nb), f32),
+            pltpu.VMEM((PIX, padded), f32),
+            pltpu.VMEM((padded, PIX), f32),
+            pltpu.VMEM((hidden, channels), bf16),
+            pltpu.VMEM((hidden, channels), bf16),
             pltpu.VMEM((2 * channels, lon_cols), bf16),
             pltpu.VMEM((lon_cols // PIX, 2 * channels, PIX), f32),
             pltpu.VMEM((2, channels, lon_cols), bf16),
@@ -417,6 +482,7 @@
             pltpu.VMEM((SLOTS, hidden), bf16),
             pltpu.VMEM((len(EDGES) * SLOTS, hidden), bf16),
             dma((1,)),
+            dma((len(held),)),
             dma((nb,)),
             dma((nb,)),
             dma((nb,)),
@@ -427,29 +493,9 @@
             dma((len(EDGES),)),
         ],
         compiler_params=pltpu.CompilerParams(
-            collective_id=0, has_side_effects=True, vmem_limit_bytes=40 << 20
+            collective_id=0, has_side_effects=True, vmem_limit_bytes=63 << 20
         ),
-    )(
-        state,
-        taps,
-        edge0,
-        edge1,
-        w_state.T,
-        w_conv.T,
-        w_adj.T,
-        bias_in[:, None],
-        w_out,
-        obs_op,
-        observations.reshape(radiance, PIX),
-        obs_mask.reshape(radiance, PIX),
-        dual_in.reshape(radiance, PIX),
-        dual_res.T,
-        dual_prev.T,
-        dual_bias[:, None],
-        dual_out_w,
-        cover,
-        pick,
-    )
+    )(state, *held, routes)
     return (state_out, dual_new.reshape(radiance, 1, PIX))
 
 

time: 52.8 us -> 40.2 us (0.76)
  the two profiles are of different devices: /device:TPU:5 before, /device:TPU:7 now
where the time goes in v3:
time: 40.2 us; the launch traced here: 40 us
  Pallas kernels  35 us (87%)
  local copies, waits for them, and re-layouts  4.4 us (11%)
  between operations  0.65 us (2%)
    pallas_call x1, Pallas kernels, on_device(): pl.pallas_call(kernel_body, out_shape=(jax.ShapeDtypeStruct(state.shape,...  35 us
    unnamed x4, local copies, waits for them, and re-layouts  4.4 us

profile of v3, /device:TPU:7, one launch (start us, length us, event | category | flops | bytes accessed | tf_op | source)
XLA Modules:
  0.0 40.0 jit_solution(1934783293351916877)
XLA Ops:
  0.6 35.0 %shard_map.167 = (bf16[822,2,512]{2,1,0:T(2,128)(2,1)}, bf16[96,128]{1,0:T(8,128)(2,1)}) custom-call(bf16[822,2,512]{2,1,0:T(2,128)(2,1)} %state.1, f32[3,3,822]{2,1,0:T(4,128)} %bitcast.22, bf16[822,256]{1,0:T(8,128)(2,1)} %bitcast.15, bf16[822,256]{1,0:T(8,128)(2,1)} %bitcast.16, bf16[822,256]{1,0:T(8,128)(2,1)} %bitcast.17, f32[1,256]{1,0:T(1,128)} %bitcast.26, ...), custom_call_target="tpu_custom_call" | custom-call | tf_op jit(solution)/shard_map/pallas_call | solution.py:453
  35.6 0.0 copy-start
  35.6 3.8 %copy.20 = bf16[822,2,512]{2,1,0:T(2,128)(2,1)} copy(bf16[822,2,512]{2,1,0:T(2,128)(2,1)} %get-tuple-element.8) | data formatting | bytes 3366912
  39.4 0.0 copy-done
  39.4 0.6 %copy.21 = bf16[96,1,128]{2,0,1:T(8,128)(2,1)} copy(bf16[96,1,128]{2,0,1:T(8,128)(2,1)S(1)} %bitcast.24) | data formatting | bytes 49152
Async XLA Ops:
  35.6 3.8 %copy-start = (bf16[96,128]{1,0:T(8,128)(2,1)S(1)}, bf16[96,128]{1,0:T(8,128)(2,1)}, u32[]{:S(2)}) copy-start(bf16[96,128]{1,0:T(8,128)(2,1)} %get-tuple-element.5) | copy-start | bytes 73732
